TPU v7x, 256 devices: a whole 4x4x8 slice. The times are simulated.
256 devices in a mesh: ctx: 32 (over x, y, core), tp: 8 (over z).
Axes of the slice: x: 4, y: 4, z: 8, core: 2. Of those that a mesh axis runs over, the one named last changes fastest.
Arguments:
- queries: bfloat16 [8192, 7168], P('ctx', 'tp'), may hold values from -6 to 6
- new_kv: bfloat16 [2, 8192, 1024], P(None, 'ctx', 'tp'), may hold values from -6 to 6
- page_cache: bfloat16 [2, 8192, 1024], P(None, 'ctx', 'tp'), may hold values from -6 to 6
- out_weight: bfloat16 [7168, 7168], P('tp', 'ctx'), may hold values from -0.5 to 0.5
- page_slot: int32 [64], replicated, may hold values from 0 to 63, each once
- parent: int32 [64], replicated, may hold values from -1 to 62, as said below
- valid_count: int32 [64], replicated, may hold values from 1 to 128
- lost_parent: int32 [64], replicated, may hold values from 0 to 63
Outputs:
- mixed: bfloat16 [8192, 7168], P('ctx', 'tp')
Inputs may be any that keep to these rules, and one draw needn't show every extreme that they name: parent[p] < p for p >= 1 and parent[0] = -1.
All inputs are finite; a program needn't handle non-finite values.
Results may differ from a plain program's by a relative error of at most 0.02.
Values may be sent and summed in bfloat16 or wider, within the bound.
A program may use at most 128 MiB of HBM per device.

v0:
```python
import math

import jax
import jax.numpy as jnp
from jax import lax
from jax.sharding import PartitionSpec as P

HEADS = 56
KV_HEADS = 8
HD = 128
PAGE = 128


def per_device(
    queries, new_kv, page_cache, out_weight, page_slot, parent, valid_count, lost_parent
):
    kv_local = page_cache.shape[2] // HD
    group_size = HEADS // KV_HEADS
    query_rows = queries.shape[0]
    pages_here = query_rows // PAGE
    surviving = parent.shape[0]
    score_scale = 1.0 / math.sqrt(HD)
    ctx_place = lax.axis_index("ctx")
    own_parents = lax.dynamic_slice_in_dim(lost_parent, ctx_place * pages_here, pages_here, 0)
    page_ids = jnp.arange(surviving, dtype=jnp.int32)
    lifted = parent + 1

    def climb(unused, state):
        current, onpath = state
        matches = current[:, None] == page_ids[None, :]
        onpath = jnp.maximum(onpath, matches.astype(jnp.float32))
        climbed = jnp.sum(jnp.where(matches, lifted[None, :], 0), axis=1) - 1
        return (climbed, onpath)

    start_state = (own_parents, jnp.zeros((pages_here, surviving), jnp.float32))
    unused_final, onpath = lax.fori_loop(0, surviving, climb, start_state)
    slot_table = (page_slot[:, None] == page_ids[None, :]).astype(jnp.float32)
    on_slot = jnp.dot(onpath, slot_table, preferred_element_type=jnp.float32)
    valid_slot = jnp.dot(
        valid_count.astype(jnp.float32)[None, :], slot_table, preferred_element_type=jnp.float32
    )[0]
    tokens = jnp.arange(PAGE, dtype=jnp.float32)
    key_mask = (on_slot[:, :, None] > 0.5) & (tokens[None, None, :] < valid_slot[None, :, None])
    key_mask = key_mask.reshape(pages_here, surviving * PAGE)
    query_heads = queries.reshape(query_rows, kv_local, group_size, HD).transpose(1, 2, 0, 3)

    def update(softmax_state, key_rows, value_rows, visible):
        running_max, weight_sum, numerator = softmax_state
        scores = (
            jnp.einsum("kgqd,nkd->kgqn", query_heads, key_rows, preferred_element_type=jnp.float32)
            * score_scale
        )
        scores = jnp.where(visible, scores, -1e30)
        new_max = jnp.maximum(running_max, jnp.max(scores, axis=-1))
        weights = jnp.exp(scores - new_max[..., None]) * visible.astype(jnp.float32)
        factor = jnp.exp(running_max - new_max)
        weight_sum = weight_sum * factor + jnp.sum(weights, axis=-1)
        numerator = numerator * factor[..., None] + jnp.einsum(
            "kgqn,nkd->kgqd",
            weights.astype(jnp.bfloat16),
            value_rows,
            preferred_element_type=jnp.float32,
        )
        return (new_max, weight_sum, numerator)

    fresh_kv = new_kv.reshape(2, query_rows, kv_local, HD)
    positions = jnp.arange(query_rows, dtype=jnp.int32)
    own_visible = (positions[None, :] // PAGE == positions[:, None] // PAGE) & (
        positions[None, :] <= positions[:, None]
    )
    start_softmax = (
        jnp.full((kv_local, group_size, query_rows), -1e30, jnp.float32),
        jnp.zeros((kv_local, group_size, query_rows), jnp.float32),
        jnp.zeros((kv_local, group_size, query_rows, HD), jnp.float32),
    )
    softmax_state = update(start_softmax, fresh_kv[0], fresh_kv[1], own_visible)
    page_piece = lax.all_gather(page_cache, "ctx", axis=1, tiled=True)
    piece_rows = page_piece.shape[1]
    block_rows = math.gcd(piece_rows, 2048)
    block_count = piece_rows // block_rows

    def one_block(number, running):
        offset = number * block_rows
        key_block = lax.dynamic_slice_in_dim(page_piece, offset, block_rows, 1).reshape(
            2, block_rows, kv_local, HD
        )
        kept_keys = lax.dynamic_slice_in_dim(key_mask, offset, block_rows, 1)
        visible = jnp.broadcast_to(kept_keys[:, None, :], (pages_here, PAGE, block_rows)).reshape(
            query_rows, block_rows
        )
        return update(running, key_block[0], key_block[1], visible)

    softmax_state = lax.fori_loop(0, block_count, one_block, softmax_state)
    running_max, weight_sum, numerator = softmax_state
    attended = (numerator / weight_sum[..., None]).transpose(2, 0, 1, 3)
    attended = attended.reshape(query_rows, kv_local * group_size * HD).astype(jnp.bfloat16)
    partial_out = jnp.dot(
        attended,
        lax.all_gather(out_weight, "ctx", axis=1, tiled=True),
        preferred_element_type=jnp.float32,
    )
    mixed = lax.psum_scatter(
        partial_out.astype(jnp.bfloat16), "tp", scatter_dimension=1, tiled=True
    )
    return mixed


def solution(mesh):
    return jax.shard_map(
        per_device,
        mesh=mesh,
        in_specs=(
            P("ctx", "tp"),
            P(None, "ctx", "tp"),
            P(None, "ctx", "tp"),
            P("tp", "ctx"),
            P(),
            P(),
            P(),
            P(),
        ),
        out_specs=P("ctx", "tp"),
        check_vma=False,
    )
```

profile of v0, /device:TPU:33, one launch (start us, length us, event | category | flops | bytes accessed | tf_op | source)
XLA Modules:
  0.0 266.4 jit_solution(12047610193651169351)
XLA Ops:
  9.5 18.1 %while.33 = (s32[]{:T(128)}, s32[2]{0:T(128)S(1)}, bf16[2,64]{1,0:T(2,128)(2,1)S(1)}, s32[64]{0:T(128)S(1)}, s32[]{:T(128)}, /*index=5*/s32[]{:T(128)}) while((s32[]{:T(128)}, s32[2]{0:T(128)S(1)}, bf16[2,64]{1,0:T(2,128)(2,1)S(1)}, s32[64]{0:T(128)S(1)}, s32[]{:T(128)}, /*index=5*/s32[]{:T(128)}) %tuple.65), condition=%wide.region_4.5_spmd.clone, body=%wide.region_2.0_spmd.clone.sunk | while | flops 1155 | bytes 895 | solution.py:36
  32.9 1.7 fusion.26
  34.7 29.7 %all-gather.3.cloned.1.call-done = bf16[2,8192,128]{2,1,0:T(8,128)(2,1)} async-done(((bf16[2,256,128]{2,1,0:T(8,128)(2,1)}), bf16[2,8192,128]{2,1,0:T(8,128)(2,1)}) %all-gather.3.cloned.1.call-update) | async-done | bytes 4194320 | tf_op jit(solution)/shard_map/all_gather | solution.py:77
  64.3 124.5 %while.32 = (s32[]{:T(128)}, f32[1,7,256]{2,1,0:T(8,128)S(1)}, f32[1,7,256]{2,1,0:T(8,128)S(1)}, f32[1,7,256,128]{3,2,1,0:T(8,128)}, pred[2,8192]{1,0:T(4,128)(4...) while((s32[]{:T(128)}, f32[1,7,256]{2,1,0:T(8,128)S(1)}, ...), condition=%wide.region_8.9_spmd, body=%wide.region_5.8_spmd.sunk | while | flops 1927746816 | bytes 61145284 | solution.py:93
  65.5 8.6 %fusion.59 = (f32[7,256]{1,0:T(8,128)S(1)}, f32[2048,7,256]{2,0,1:T(8,128)}) fusion(pred[256,2048]{0,1:T(8,128)(4,1)S(1)} %copy.37, bf16[1,7,256,128]{3,2,1,0:T(8,128)(2,1)S(1)} %get-tuple-element.386, bf16[2,8192,128]{2,1,0:T(8,128)(2,1)} %get-tuple-element.385, s32[]{:T(128)S(6)} %select_n.92), kind=kOutput, calls=%fused_computation.3.clone.1 | convolution fusion | flops 950532352 | bytes 16194564 | tf_op jit(solution)/shard_map/while/body/eval_jaxpr/kgqd,nkd->kgqn/dot_general | solution.py:50
  75.6 1.9 copy.38
  77.6 9.0 %fusion.61 = f32[7,256]{1,0:T(8,128)S(1)} fusion(f32[2048,7,256]{2,0,1:T(8,128)} %get-tuple-element.332, f32[256,2048]{0,1:T(8,128)S(1)} %copy.38, f32[7,256]{1,0:T(8,128)S(1)} %bitcast.116, pred[256,2048]{0,1:T(8,128)(4,1)S(1)} %copy.37), kind=kLoop, calls=%fused_computation.5.clone.1 | loop fusion | flops 18348288 | bytes 17315840 | tf_op jit(solution)/shard_map/while/body/eval_jaxpr/reduce_sum | solution.py:57
  86.6 8.8 %fusion.62 = f32[1,7,256,128]{3,2,1,0:T(8,128)} fusion(f32[2048,7,256]{2,0,1:T(8,128)} %get-tuple-element.332, f32[256,2048]{0,1:T(8,128)S(1)} %copy.38, f32[7,256]{1,0:T(8,128)S(1)} %bitcast.117, pred[256,2048]{0,1:T(8,128)(4,1)S(1)} %copy.37, f32[1,7,256,128]{3,2,1,0:T(8,128)} %get-tuple-element.371, bf16[2,8192,128]{2,1,0:T(8,128)(2,1)} %get-tuple-element.385, ...), kind=kOutput, calls=%fused_computation.9.clone.1 | convolution fusion | flops 958332928 | bytes 19675144 | tf_op jit(solution)/shard_map/while/body/eval_jaxpr/kgqn,nkd->kgqd/dot_general | solution.py:58
  96.5 9.3 %fusion.59 = (f32[7,256]{1,0:T(8,128)S(1)}, f32[2048,7,256]{2,0,1:T(8,128)}) fusion(pred[256,2048]{0,1:T(8,128)(4,1)S(1)} %copy.37, bf16[1,7,256,128]{3,2,1,0:T(8,128)(2,1)S(1)} %get-tuple-element.386, bf16[2,8192,128]{2,1,0:T(8,128)(2,1)} %get-tuple-element.385, s32[]{:T(128)S(6)} %select_n.92), kind=kOutput, calls=%fused_computation.3.clone.1 | convolution fusion | flops 950532352 | bytes 16194564 | tf_op jit(solution)/shard_map/while/body/eval_jaxpr/kgqd,nkd->kgqn/dot_general | solution.py:50
  107.3 1.9 copy.38
  109.3 9.2 %fusion.61 = f32[7,256]{1,0:T(8,128)S(1)} fusion(f32[2048,7,256]{2,0,1:T(8,128)} %get-tuple-element.332, f32[256,2048]{0,1:T(8,128)S(1)} %copy.38, f32[7,256]{1,0:T(8,128)S(1)} %bitcast.116, pred[256,2048]{0,1:T(8,128)(4,1)S(1)} %copy.37), kind=kLoop, calls=%fused_computation.5.clone.1 | loop fusion | flops 18348288 | bytes 17315840 | tf_op jit(solution)/shard_map/while/body/eval_jaxpr/reduce_sum | solution.py:57
  118.5 9.2 %fusion.62 = f32[1,7,256,128]{3,2,1,0:T(8,128)} fusion(f32[2048,7,256]{2,0,1:T(8,128)} %get-tuple-element.332, f32[256,2048]{0,1:T(8,128)S(1)} %copy.38, f32[7,256]{1,0:T(8,128)S(1)} %bitcast.117, pred[256,2048]{0,1:T(8,128)(4,1)S(1)} %copy.37, f32[1,7,256,128]{3,2,1,0:T(8,128)} %get-tuple-element.371, bf16[2,8192,128]{2,1,0:T(8,128)(2,1)} %get-tuple-element.385, ...), kind=kOutput, calls=%fused_computation.9.clone.1 | convolution fusion | flops 958332928 | bytes 19675144 | tf_op jit(solution)/shard_map/while/body/eval_jaxpr/kgqn,nkd->kgqd/dot_general | solution.py:58
  128.9 8.6 %fusion.59 = (f32[7,256]{1,0:T(8,128)S(1)}, f32[2048,7,256]{2,0,1:T(8,128)}) fusion(pred[256,2048]{0,1:T(8,128)(4,1)S(1)} %copy.37, bf16[1,7,256,128]{3,2,1,0:T(8,128)(2,1)S(1)} %get-tuple-element.386, bf16[2,8192,128]{2,1,0:T(8,128)(2,1)} %get-tuple-element.385, s32[]{:T(128)S(6)} %select_n.92), kind=kOutput, calls=%fused_computation.3.clone.1 | convolution fusion | flops 950532352 | bytes 16194564 | tf_op jit(solution)/shard_map/while/body/eval_jaxpr/kgqd,nkd->kgqn/dot_general | solution.py:50
  139.0 1.9 copy.38
  141.0 8.6 %fusion.61 = f32[7,256]{1,0:T(8,128)S(1)} fusion(f32[2048,7,256]{2,0,1:T(8,128)} %get-tuple-element.332, f32[256,2048]{0,1:T(8,128)S(1)} %copy.38, f32[7,256]{1,0:T(8,128)S(1)} %bitcast.116, pred[256,2048]{0,1:T(8,128)(4,1)S(1)} %copy.37), kind=kLoop, calls=%fused_computation.5.clone.1 | loop fusion | flops 18348288 | bytes 17315840 | tf_op jit(solution)/shard_map/while/body/eval_jaxpr/reduce_sum | solution.py:57
  149.6 8.7 %fusion.62 = f32[1,7,256,128]{3,2,1,0:T(8,128)} fusion(f32[2048,7,256]{2,0,1:T(8,128)} %get-tuple-element.332, f32[256,2048]{0,1:T(8,128)S(1)} %copy.38, f32[7,256]{1,0:T(8,128)S(1)} %bitcast.117, pred[256,2048]{0,1:T(8,128)(4,1)S(1)} %copy.37, f32[1,7,256,128]{3,2,1,0:T(8,128)} %get-tuple-element.371, bf16[2,8192,128]{2,1,0:T(8,128)(2,1)} %get-tuple-element.385, ...), kind=kOutput, calls=%fused_computation.9.clone.1 | convolution fusion | flops 958332928 | bytes 19675144 | tf_op jit(solution)/shard_map/while/body/eval_jaxpr/kgqn,nkd->kgqd/dot_general | solution.py:58
  159.5 8.6 %fusion.59 = (f32[7,256]{1,0:T(8,128)S(1)}, f32[2048,7,256]{2,0,1:T(8,128)}) fusion(pred[256,2048]{0,1:T(8,128)(4,1)S(1)} %copy.37, bf16[1,7,256,128]{3,2,1,0:T(8,128)(2,1)S(1)} %get-tuple-element.386, bf16[2,8192,128]{2,1,0:T(8,128)(2,1)} %get-tuple-element.385, s32[]{:T(128)S(6)} %select_n.92), kind=kOutput, calls=%fused_computation.3.clone.1 | convolution fusion | flops 950532352 | bytes 16194564 | tf_op jit(solution)/shard_map/while/body/eval_jaxpr/kgqd,nkd->kgqn/dot_general | solution.py:50
  169.6 1.9 copy.38
  171.5 8.6 %fusion.61 = f32[7,256]{1,0:T(8,128)S(1)} fusion(f32[2048,7,256]{2,0,1:T(8,128)} %get-tuple-element.332, f32[256,2048]{0,1:T(8,128)S(1)} %copy.38, f32[7,256]{1,0:T(8,128)S(1)} %bitcast.116, pred[256,2048]{0,1:T(8,128)(4,1)S(1)} %copy.37), kind=kLoop, calls=%fused_computation.5.clone.1 | loop fusion | flops 18348288 | bytes 17315840 | tf_op jit(solution)/shard_map/while/body/eval_jaxpr/reduce_sum | solution.py:57
  180.2 8.7 %fusion.62 = f32[1,7,256,128]{3,2,1,0:T(8,128)} fusion(f32[2048,7,256]{2,0,1:T(8,128)} %get-tuple-element.332, f32[256,2048]{0,1:T(8,128)S(1)} %copy.38, f32[7,256]{1,0:T(8,128)S(1)} %bitcast.117, pred[256,2048]{0,1:T(8,128)(4,1)S(1)} %copy.37, f32[1,7,256,128]{3,2,1,0:T(8,128)} %get-tuple-element.371, bf16[2,8192,128]{2,1,0:T(8,128)(2,1)} %get-tuple-element.385, ...), kind=kOutput, calls=%fused_computation.9.clone.1 | convolution fusion | flops 958332928 | bytes 19675144 | tf_op jit(solution)/shard_map/while/body/eval_jaxpr/kgqn,nkd->kgqd/dot_general | solution.py:58
  190.4 14.5 %convolution_convert_fusion = bf16[256,7168]{1,0:T(8,128)(2,1)} fusion(bf16[256,896]{0,1:T(8,128)(2,1)S(1)} %bitcast.119, bf16[896,7168]{0,1:T(8,128)(2,1)} %all-gather.5.cloned.1.call-done), kind=kOutput, calls=%fused_computation.30 | convolution fusion | flops 3290169344 | bytes 16973824 | tf_op jit(solution)/shard_map/dot_general | solution.py:97
  204.9 5.9 %copy.31 = bf16[256,7168]{0,1:T(8,128)(2,1)} copy(bf16[256,7168]{1,0:T(8,128)(2,1)} %convolution_convert_fusion) | data formatting | bytes 7340032
  210.9 47.0 %reduce-scatter.4.cloned.1.call-done = bf16[896,256]{1,0:T(8,128)(2,1)} async-done(((bf16[7168,256]{1,0:T(8,128)(2,1)}), bf16[896,256]{1,0:T(8,128)(2,1)}) %reduce-scatter.4.cloned.1.call-update) | async-done | bytes 458768
  257.9 2.0 copy.32
  (248 shorter events, 37.8 us)
Async XLA Ops:
  6.5 26.4 %copy-start = (bf16[2,256,128]{2,1,0:T(8,128)(2,1)S(1)}, bf16[2,256,128]{2,1,0:T(8,128)(2,1)}, u32[]{:S(2)}) copy-start(bf16[2,256,128]{2,1,0:T(8,128)(2,1)} %param.13) | copy-start | bytes 393220
  6.5 57.8 %all-gather.3.cloned.1.call-start = ((), (), s32[]{:S(2)}) async-start(), calls=%async_computation.1 | async-start | bytes 4325376 | tf_op jit(solution)/shard_map/all_gather | solution.py:77
  7.3 183.2 %all-gather.5.cloned.1.call-start = ((), (), s32[]{:S(2)}) async-start(), calls=%async_computation.2 | async-start | bytes 13246464 | tf_op jit(solution)/shard_map/all_gather | solution.py:99
  8.0 249.9 %reduce-scatter.4.cloned.1.call-start = ((), (), s32[]{:S(2)}) async-start(), calls=%async_computation.3 | async-start | bytes 4128768
Sparse Core Ops, SparseCore 0:
  10.0 54.2 all-gather.2
  66.9 67.8 all-gather.4
  211.0 46.8 reduce-scatter.3
where the time goes:
time: 271 us; the launch traced here: 266 us
  matrix products  89.5 us (33%)
  waiting for transfers between devices  78.1 us (29%)
  other arithmetic  60.1 us (22%)
  local copies, waits for them, and re-layouts  24.2 us (9%)
  between operations  13.2 us (5%)
    unnamed x4, waiting for transfers between devices  48.5 us
    dot_general x5, matrix products, update(): jnp.einsum('kgqn,nkd->kgqd', weights.astype(jnp.bfloat16), value_rows, pr...  37 us
    dot_general x5, matrix products, update(): jnp.einsum('kgqd,nkd->kgqn', query_heads, key_rows, preferred_element_typ...  36.3 us
    reduce_sum x5, other arithmetic, update(): weight_sum = weight_sum * factor + jnp.sum(weights, axis=-1)  35.9 us
    all_gather x1, waiting for transfers between devices, per_device(): page_piece = lax.all_gather(page_cache, 'ctx', axis=1, tiled=True)  29.7 us
    dot_general x1, matrix products, per_device(): jnp.dot(attended, lax.all_gather(out_weight, 'ctx', axis=1, tiled=True),...  14.5 us
    reduce_sum x64, other arithmetic, climb(): climbed = jnp.sum(jnp.where(matches, lifted[None, :], 0), axis=1) - 1  11.6 us
    unnamed x6, local copies, waits for them, and re-layouts  9.24 us
  transfers between devices with their start and end apart: 3, of which 2 were waited for; matrix products, arithmetic and copies ran while one was open for 57% of the time, Pallas kernels for 0%

commit v1 on v0

v1 whole, which is shorter than its diff:
```python
import math

import jax
import jax.numpy as jnp
from jax import lax
from jax.experimental import pallas as pl
from jax.experimental.pallas import tpu as pltpu
from jax.sharding import PartitionSpec as P

HEADS = 56
KV_HEADS = 8
HD = 128
PAGE = 128
GROUP = HEADS // KV_HEADS
CHUNK = 512
MESH = pl.DeviceIdType.MESH
VMEM_LIMIT = 56 * 2**20


def place():
    c = lax.axis_index("ctx")
    return lax.div(c, 8), lax.rem(lax.div(c, 2), 4), lax.rem(c, 2), lax.axis_index("tp")


def ctx_of(x, y, k):
    return (x * 4 + y) * 2 + k


def gather_kernel(page_ref, kv_ref, own_sem, send1, recv1, send2, recv2, core_send, core_recv):
    x, y, k, t = place()

    def at_x(d):
        return (ctx_of(lax.rem(x + d, 4), y, k), t)

    def at_y(d):
        return (ctx_of(x, lax.rem(y + d, 4), k), t)

    other = (ctx_of(x, y, 1 - k), t)
    barrier = pltpu.get_barrier_semaphore()
    for d in (1, 2, 3):
        pl.semaphore_signal(barrier, inc=1, device_id=at_x(d), device_id_type=MESH)
        pl.semaphore_signal(barrier, inc=1, device_id=at_y(d), device_id_type=MESH)
    pl.semaphore_signal(barrier, inc=1, device_id=other, device_id_type=MESH)
    own = pltpu.make_async_copy(page_ref, kv_ref.at[:, x, y, k], own_sem)
    own.start()
    pl.semaphore_wait(barrier, 7)

    def remote(src, dst, send, recv, device):
        return pltpu.make_async_remote_copy(
            src, dst, send, recv, device_id=device, device_id_type=MESH
        )

    first = {}
    for d in (2, 1, 3):
        first[0, d] = remote(page_ref.at[0], kv_ref.at[0, x, y, k], send1.at[0, d], recv1.at[0, d], at_x(d))
        first[1, d] = remote(page_ref.at[1], kv_ref.at[1, x, y, k], send1.at[1, d], recv1.at[1, d], at_y(d))
        first[0, d].start()
        first[1, d].start()
    own.wait()
    for d in (1, 3, 2):
        first[0, d].wait_recv()
        first[1, d].wait_recv()
    row_block = kv_ref.at[0, :, y, k]
    column_block = kv_ref.at[1, x, :, k]
    second = {}
    for d in (2, 1, 3):
        second[0, d] = remote(row_block, row_block, send2.at[0, d], recv2.at[0, d], at_y(d))
        second[1, d] = remote(column_block, column_block, send2.at[1, d], recv2.at[1, d], at_x(d))
        second[0, d].start()
        second[1, d].start()
    shared = []
    for part, block in ((0, row_block), (1, column_block)):
        copy = remote(block, block, core_send.at[part, 0], core_recv.at[part, 0], other)
        copy.start()
        shared.append(copy)
    for d in (1, 3, 2):
        second[0, d].wait_recv()
        block = kv_ref.at[0, :, lax.rem(y + 4 - d, 4), k]
        copy = remote(block, block, core_send.at[0, d], core_recv.at[0, d], other)
        copy.start()
        shared.append(copy)
        second[1, d].wait_recv()
        block = kv_ref.at[1, lax.rem(x + 4 - d, 4), :, k]
        copy = remote(block, block, core_send.at[1, d], core_recv.at[1, d], other)
        copy.start()
        shared.append(copy)
    for copy in shared:
        copy.wait()
    for copy in list(first.values()) + list(second.values()):
        copy.wait_send()


def gather_pages(page_cache):
    rows = page_cache.shape[1]
    return pl.pallas_call(
        gather_kernel,
        out_shape=jax.ShapeDtypeStruct((2, 4, 4, 2, rows, HD), jnp.bfloat16),
        in_specs=[pl.BlockSpec(memory_space=pl.ANY)],
        out_specs=pl.BlockSpec(memory_space=pl.ANY),
        scratch_shapes=[pltpu.SemaphoreType.DMA(())]
        + [pltpu.SemaphoreType.DMA((2, 4))] * 6,
        compiler_params=pltpu.CompilerParams(collective_id=0, has_side_effects=True),
        name="gather_pages",
    )(page_cache)


def attention_kernel(
    slot_ref, parent_ref, count_ref, lost_ref, q_ref, new_ref, kv_ref, out_ref, keys, values, query, top, total
):
    pages_here = q_ref.shape[0] // PAGE
    scale = math.log2(math.e) / math.sqrt(HD)
    base = lax.axis_index("ctx") * pages_here
    token = lax.broadcasted_iota(jnp.int32, (PAGE, HD), 0)
    nt = (((1,), (1,)), ((), ()))

    def one_lost(j, unused):
        rows = pl.ds(pl.multiple_of(j * PAGE, PAGE), PAGE)

        def append(state):
            page, filled = state
            count = count_ref[page]
            at = pl.ds(pl.multiple_of(slot_ref[page] * PAGE, PAGE), PAGE)
            to = pl.ds(pl.multiple_of(filled, 16), PAGE)
            kept = token < count
            key = kv_ref[0, at, :].astype(jnp.float32)
            keys[to, :] = jnp.where(kept, key, key[:1, :]).astype(jnp.bfloat16)
            value = kv_ref[1, at, :].astype(jnp.float32)
            values[to, :HD] = jnp.where(kept, value, 0.0).astype(jnp.bfloat16)
            values[to, HD:] = kept.astype(jnp.float32).astype(jnp.bfloat16)
            return parent_ref[page], filled + ((count + 15) // 16) * 16

        unused_page, filled = lax.while_loop(
            lambda state: state[0] >= 0, append, (lost_ref[base + j], jnp.int32(0))
        )
        tail = pl.ds(pl.multiple_of(filled, 16), CHUNK)
        keys[tail, :] = jnp.broadcast_to(keys[:1, :].astype(jnp.float32), (CHUNK, HD)).astype(jnp.bfloat16)
        values[tail, :] = jnp.zeros((CHUNK, 2 * HD), jnp.bfloat16)
        for h in range(GROUP):
            query[h * PAGE : (h + 1) * PAGE, :] = q_ref[rows, h * HD : (h + 1) * HD]

        fresh = lax.dot_general(query[...], new_ref[0, rows, :], nt, preferred_element_type=jnp.float32) * scale
        q_at = lax.rem(lax.broadcasted_iota(jnp.int32, (GROUP * PAGE, PAGE), 0), PAGE)
        k_at = lax.broadcasted_iota(jnp.int32, (GROUP * PAGE, PAGE), 1)
        seen = k_at <= q_at
        fresh = jnp.where(seen, fresh, -1e30)
        highest = jnp.max(fresh, axis=1, keepdims=True)
        weight = jnp.where(seen, jnp.exp2(fresh - highest), 0.0).astype(jnp.bfloat16)
        with_ones = jnp.concatenate([new_ref[1, rows, :], jnp.ones((PAGE, HD), jnp.bfloat16)], axis=1)
        top[...] = jnp.broadcast_to(highest, top.shape)
        total[...] = jnp.dot(weight, with_ones, preferred_element_type=jnp.float32)

        def one_chunk(n, unused):
            at = pl.ds(pl.multiple_of(n * CHUNK, CHUNK), CHUNK)
            score = lax.dot_general(query[...], keys[at, :], nt, preferred_element_type=jnp.float32) * scale
            before = top[:, :1]
            highest = jnp.maximum(before, jnp.max(score, axis=1, keepdims=True))
            weight = jnp.exp2(score - highest).astype(jnp.bfloat16)
            factor = jnp.exp2(before - highest)
            top[...] = jnp.broadcast_to(highest, top.shape)
            total[...] = total[...] * factor + jnp.dot(weight, values[at, :], preferred_element_type=jnp.float32)
            return unused

        lax.fori_loop(0, (filled + CHUNK - 1) // CHUNK, one_chunk, 0)
        for h in range(GROUP):
            block = total[h * PAGE : (h + 1) * PAGE, :]
            out_ref[rows, h * HD : (h + 1) * HD] = (block[:, :HD] / block[:, HD:]).astype(jnp.bfloat16)
        return unused

    lax.fori_loop(0, pages_here, one_lost, 0)


def attend(queries, new_kv, kv, page_slot, parent, valid_count, lost_parent):
    rows = kv.shape[1]
    smem = pl.BlockSpec(memory_space=pltpu.SMEM)
    vmem = pl.BlockSpec(memory_space=pltpu.VMEM)
    return pl.pallas_call(
        attention_kernel,
        out_shape=jax.ShapeDtypeStruct(queries.shape, jnp.bfloat16),
        in_specs=[smem] * 4 + [vmem] * 3,
        out_specs=vmem,
        scratch_shapes=[
            pltpu.VMEM((rows + CHUNK, HD), jnp.bfloat16),
            pltpu.VMEM((rows + CHUNK, 2 * HD), jnp.bfloat16),
            pltpu.VMEM((GROUP * PAGE, HD), jnp.bfloat16),
            pltpu.VMEM((GROUP * PAGE, HD), jnp.float32),
            pltpu.VMEM((GROUP * PAGE, 2 * HD), jnp.float32),
        ],
        compiler_params=pltpu.CompilerParams(vmem_limit_bytes=VMEM_LIMIT),
        name="attend",
    )(page_slot, parent, valid_count, lost_parent, queries, new_kv, kv)


ORDER = [(0, 0), (1, 0), (0, 1), (1, 1), (0, 2), (1, 2)]
for _s in range(8):
    ORDER += [(2, _s), (3, _s)]
    if _s + 3 < 8:
        ORDER += [(0, _s + 3), (1, _s + 3)]


def project_kernel(
    att_ref, w_ref, out_ref, peers, outgoing, incoming, final, a_send, a_recv, z_send, z_recv, f_send, f_recv
):
    x, y, k, t = place()
    y_other = y + 1 - 2 * lax.rem(y, 2)
    mine = lax.rem(y, 2) * 2 + k
    holder = {
        1: (ctx_of(x, y, 1 - k), t),
        2: (ctx_of(x, y_other, k), t),
        3: (ctx_of(x, y_other, 1 - k), t),
    }
    here = ctx_of(x, y, k)
    barrier = pltpu.get_barrier_semaphore()
    for device in list(holder.values()) + [(here, lax.rem(t + 1, 8)), (here, lax.rem(t + 7, 8))]:
        pl.semaphore_signal(barrier, inc=1, device_id=device, device_id_type=MESH)
    pl.semaphore_wait(barrier, 5)

    def remote(src, dst, send, recv, device):
        copy = pltpu.make_async_remote_copy(src, dst, send, recv, device_id=device, device_id_type=MESH)
        copy.start()
        return copy

    shares = {
        1: remote(att_ref, peers.at[0], a_send.at[0], a_recv.at[0], holder[1]),
        2: remote(att_ref, peers.at[1], a_send.at[1], a_recv.at[1], holder[2]),
    }
    step_of = {0: 1 - 2 * k, 1: 2 * k - 1, 2: 1 - 2 * k, 3: 2 * k - 1}
    columns = w_ref.shape[1]
    nt = (((1,), (1,)), ((), ()))
    hops = {}
    finals = []
    for block, s in ORDER:
        if s == 0 and block > 0:
            shares[block].wait_recv()
            if block == 2:
                shares[3] = remote(peers.at[1], peers.at[2], a_send.at[2], a_recv.at[2], holder[1])
        step = step_of[block]
        target = lax.rem(t - step * (1 + s) + 16, 8)
        rows = att_ref[...] if block == 0 else peers[block - 1]
        term = lax.dot_general(w_ref[target], rows, nt, preferred_element_type=jnp.float32)
        if s > 0:
            hops[block, s - 1].wait_recv()
            term = term + incoming[block, s - 1].astype(jnp.float32)
        term = term.astype(jnp.bfloat16)
        if s < 7:
            outgoing[block, s] = term
            hops[block, s] = remote(
                outgoing.at[block, s],
                incoming.at[block, s],
                z_send.at[block, s],
                z_recv.at[block, s],
                (here, lax.rem(t + step + 8, 8)),
            )
        else:
            spot = pl.ds(pl.multiple_of(mine * columns, 16), columns)
            if block == 0:
                out_ref[spot, :] = term
            else:
                final[block - 1] = term
                finals.append(
                    remote(
                        final.at[block - 1],
                        out_ref.at[spot, :],
                        f_send.at[block - 1],
                        f_recv.at[block - 1],
                        holder[block],
                    )
                )
    for copy in finals:
        copy.wait()
    for copy in list(shares.values()) + list(hops.values()):
        copy.wait_send()


def project(attended, weights):
    rows, depth = attended.shape
    parts, columns, _ = weights.shape
    vmem = pl.BlockSpec(memory_space=pltpu.VMEM)
    return pl.pallas_call(
        project_kernel,
        out_shape=jax.ShapeDtypeStruct((4 * columns, rows), jnp.bfloat16),
        in_specs=[vmem, vmem],
        out_specs=vmem,
        scratch_shapes=[
            pltpu.VMEM((3, rows, depth), jnp.bfloat16),
            pltpu.VMEM((4, 7, columns, rows), jnp.bfloat16),
            pltpu.VMEM((4, 7, columns, rows), jnp.bfloat16),
            pltpu.VMEM((3, columns, rows), jnp.bfloat16),
            pltpu.SemaphoreType.DMA((3,)),
            pltpu.SemaphoreType.DMA((3,)),
            pltpu.SemaphoreType.DMA((4, 7)),
            pltpu.SemaphoreType.DMA((4, 7)),
            pltpu.SemaphoreType.DMA((3,)),
            pltpu.SemaphoreType.DMA((3,)),
        ],
        compiler_params=pltpu.CompilerParams(
            collective_id=1, has_side_effects=True, vmem_limit_bytes=VMEM_LIMIT
        ),
        name="project",
    )(attended, weights)


def weight_groups():
    return [
        [(x * 4 + high * 2 + low) * 2 + k for x in range(4) for high in range(2)]
        for low in range(2)
        for k in range(2)
    ]


def per_device(
    queries, new_kv, page_cache, out_weight, page_slot, parent, valid_count, lost_parent
):
    weights = lax.all_gather(out_weight.T, "ctx", axis_index_groups=weight_groups())
    kv = gather_pages(page_cache).reshape(2, -1, HD)
    attended = attend(queries, new_kv, kv, page_slot, parent, valid_count, lost_parent)
    return project(attended, weights).T


def solution(mesh):
    return jax.shard_map(
        per_device,
        mesh=mesh,
        in_specs=(
            P("ctx", "tp"),
            P(None, "ctx", "tp"),
            P(None, "ctx", "tp"),
            P("tp", "ctx"),
            P(),
            P(),
            P(),
            P(),
        ),
        out_specs=P("ctx", "tp"),
        check_vma=False,
    )
```

time: 271 us -> 153 us (0.56)
  Pallas kernels: 0 us -> 105 us
  matrix products: 89.5 us -> 0 us
  other arithmetic: 60.1 us -> 0 us
  waiting for transfers between devices: 78.1 us -> 29.8 us
  local copies, waits for them, and re-layouts: 24.2 us -> 1.99 us
    pallas_call x0 -> x3, Pallas kernels: none -> 105 us  [the longest x1 59.2 us: project(): pl.pallas_call(project_kernel, out_shape=jax.ShapeDtypeStruct((4 * column...]
    dot_general x13 -> x0, matrix products: 89.5 us -> none  [the longest x5 37 us: update(): jnp.einsum('kgqn,nkd->kgqd', weights.astype(jnp.bfloat16), value_rows, pr...]
    unnamed x4 -> x1, waiting for transfers between devices: 48.5 us -> 0.71 us
    reduce_sum x69 -> x0, other arithmetic: 47.5 us -> none  [the longest x5 35.9 us: update(): weight_sum = weight_sum * factor + jnp.sum(weights, axis=-1)]
    unnamed x6 -> x0, local copies, waits for them, and re-layouts: 9.24 us -> none
    convert_element_type x4 -> x0, local copies, waits for them, and re-layouts: 7.68 us -> none  [update(): weights = jnp.exp(scores - new_max[..., None]) * visible.astype(jnp.float32)]
    convert_element_type x6 -> x0, other arithmetic: 6.19 us -> none  [the longest x5 6.11 us: update(): weights = jnp.exp(scores - new_max[..., None]) * visible.astype(jnp.float32)]
    max x64 -> x0, other arithmetic: 5.15 us -> none  [climb(): onpath = jnp.maximum(onpath, matches.astype(jnp.float32))]
  transfers between devices with their start and end apart: 3 -> 1, of which waited for: 2 -> 1; matrix products, arithmetic and copies ran while one was open for 57% -> 0% of each run, Pallas kernels for 0% -> 30%
where the time goes in v1:
time: 153 us; the launch traced here: 150 us
  Pallas kernels  105 us (69%)
  waiting for transfers between devices  29.8 us (19%)
  between operations  13.4 us (9%)
  local copies, waits for them, and re-layouts  1.99 us (1%)
    pallas_call x1, Pallas kernels, project(): pl.pallas_call(project_kernel, out_shape=jax.ShapeDtypeStruct((4 * column...  59.2 us
    all_gather x1, waiting for transfers between devices, per_device(): lax.all_gather(out_weight.T, 'ctx', axis_index_groups=weight_groups())  29.1 us
    pallas_call x1, Pallas kernels, gather_pages(): pl.pallas_call(gather_kernel, out_shape=jax.ShapeDtypeStruct((2, 4, 4, 2,...  28.5 us
    pallas_call x1, Pallas kernels, attend(): pl.pallas_call(attention_kernel, out_shape=jax.ShapeDtypeStruct(queries.s...  17 us
  transfers between devices with their start and end apart: 1, of which 1 were waited for; matrix products, arithmetic and copies ran while one was open for 0% of the time, Pallas kernels for 30%

profile of v1, /device:TPU:33, one launch (start us, length us, event | category | flops | bytes accessed | tf_op | source)
XLA Modules:
  0.0 149.9 jit_solution(10800112192010018125)
XLA Ops:
  6.5 0.0 all-gather.3.cloned.1.call-start
  6.5 0.7 all-gather.3.cloned.1.call-update
  7.3 28.5 %gather_pages.1 = bf16[2,4,4,2,256,128]{5,4,3,2,1,0:T(8,128)(2,1)} custom-call(bf16[2,256,128]{2,1,0:T(8,128)(2,1)} %page_ref.1), custom_call_target="tpu_custom_call" | custom-call | tf_op jit(solution)/shard_map/gather_pages/pallas_call | solution.py:95
  35.7 17.0 %attend.1.att_ref = bf16[256,896]{1,0:T(8,128)(2,1)} custom-call(s32[64]{0:T(128)} %slot_ref.1, s32[64]{0:T(128)} %parent_ref.1, s32[64]{0:T(128)} %count_ref.1, s32[64]{0:T(128)} %lost_ref.1, bf16[256,896]{1,0:T(8,128)(2,1)} %q_ref.1, bf16[2,256,128]{2,1,0:T(8,128)(2,1)} %new_ref.1, bf16[2,8192,128]{2,1,0:T(8,128)(2,1)} %bitcast.4), custom_call_target="tpu_custom_call" | custom-call | tf_op jit(solution)/shard_map/attend/pallas_call | solution.py:176
  52.7 29.1 %all-gather.3.cloned.1.call-done = bf16[1792,896]{1,0:T(8,128)(2,1)} async-done(((bf16[224,896]{1,0:T(8,128)(2,1)}), bf16[1792,896]{1,0:T(8,128)(2,1)}) %all-gather.3.cloned.1.call-update) | async-done | bytes 3211280 | tf_op jit(solution)/shard_map/all_gather | solution.py:313
  81.8 59.2 %project.1 = bf16[896,256]{1,0:T(8,128)(2,1)} custom-call(bf16[256,896]{1,0:T(8,128)(2,1)} %attend.1.att_ref, bf16[8,224,896]{2,1,0:T(8,128)(2,1)} %bitcast.5), custom_call_target="tpu_custom_call" | custom-call | tf_op jit(solution)/shard_map/project/pallas_call | solution.py:278
  141.1 2.0 %copy.9 = bf16[256,896]{1,0:T(8,128)(2,1)} copy(bf16[256,896]{0,1:T(8,128)(2,1)} %bitcast.6) | data formatting | bytes 917504 | tf_op jit(solution)/shard_map/transpose | solution.py:316
Async XLA Ops:
  6.5 75.3 %all-gather.3.cloned.1.call-start = ((), (), s32[]{:S(2)}) async-start(), calls=%async_computation | async-start | bytes 3612672 | tf_op jit(solution)/shard_map/all_gather | solution.py:313
Sparse Core Ops, SparseCore 0:
  10.0 71.8 all-gather.2

commit v2 on v1

v2 whole, which is shorter than its diff:
```python
import math

import jax
import jax.numpy as jnp
from jax import lax
from jax.experimental import pallas as pl
from jax.experimental.pallas import tpu as pltpu
from jax.sharding import PartitionSpec as P

HEADS = 56
KV_HEADS = 8
HD = 128
PAGE = 128
GROUP = HEADS // KV_HEADS
CHUNK = 512
MESH = pl.DeviceIdType.MESH
VMEM_LIMIT = 28 * 2**20


def place():
    c = lax.axis_index("ctx")
    return lax.div(c, 8), lax.rem(lax.div(c, 2), 4), lax.rem(c, 2), lax.axis_index("tp")


def ctx_of(x, y, k):
    return (x * 4 + y) * 2 + k


def gather_kernel(page_ref, w_ref, kv_ref, wall_ref, own_sem, send_sem, recv_sem):
    x, y, k, t = place()

    def at_x(d):
        return (ctx_of(lax.rem(x + d, 4), y, k), t)

    def at_y(d):
        return (ctx_of(x, lax.rem(y + d, 4), k), t)

    other = (ctx_of(x, y, 1 - k), t)
    barrier = pltpu.get_barrier_semaphore()
    for device in (at_x(1), at_x(2), at_x(3), at_y(1), at_y(3), other):
        pl.semaphore_signal(barrier, inc=1, device_id=device, device_id_type=MESH)
    own = [
        pltpu.make_async_copy(page_ref, kv_ref.at[:, x, y, k], own_sem.at[0]),
        pltpu.make_async_copy(w_ref, wall_ref.at[x], own_sem.at[1]),
    ]
    for copy in own:
        copy.start()
    pl.semaphore_wait(barrier, 6)

    copies = []

    def remote(src, dst, device):
        n = len(copies)
        copy = pltpu.make_async_remote_copy(
            src, dst, send_sem.at[n], recv_sem.at[n], device_id=device, device_id_type=MESH
        )
        copy.start()
        copies.append(copy)
        return copy

    def piece(dx, dy):
        return kv_ref.at[:, lax.rem(x + dx, 4), lax.rem(y + dy, 4), k]

    def half(part, dx, dy):
        return kv_ref.at[part, lax.rem(x + dx, 4), lax.rem(y + dy, 4), k]

    home = piece(0, 0)
    along = {d: remote(page_ref, home, at_x(d)) for d in (1, 3, 2)}
    up = {0: remote(page_ref, home, at_y(1))}
    down = {0: remote(page_ref, home, at_y(3))}
    shared = [remote(page_ref, home, other)]
    for d in (1, 3, 2):
        along[d].wait_recv()
        here = piece(4 - d, 0)
        up[d] = remote(here, here, at_y(1))
        down[d] = remote(here, here, at_y(3))
        shared.append(remote(here, here, other))
    right = remote(w_ref, wall_ref.at[x], at_x(1))
    left = remote(w_ref, wall_ref.at[x], at_x(3))
    far = {}
    far_w = []
    middle = w_ref.shape[0] // 2
    for d in (0, 1, 3, 2):
        dx = (4 - d) % 4
        up[d].wait_recv()
        here = half(0, dx, 3)
        far[0, d] = remote(here, here, at_y(1))
        shared.append(remote(piece(dx, 3), piece(dx, 3), other))
        down[d].wait_recv()
        here = half(1, dx, 1)
        far[1, d] = remote(here, here, at_y(3))
        shared.append(remote(piece(dx, 1), piece(dx, 1), other))
        if d == 3:
            right.wait_recv()
            here = wall_ref.at[lax.rem(x + 3, 4), pl.ds(0, middle)]
            far_w.append(remote(here, here, at_x(1)))
            left.wait_recv()
            here = wall_ref.at[lax.rem(x + 1, 4), pl.ds(middle, middle)]
            far_w.append(remote(here, here, at_x(3)))
    for d in (0, 1, 3, 2):
        far[0, d].wait_recv()
        far[1, d].wait_recv()
        here = piece((4 - d) % 4, 2)
        shared.append(remote(here, here, other))
    for copy in far_w:
        copy.wait_recv()
    for copy in shared:
        copy.wait_recv()
    for copy in copies:
        copy.wait_send()
    for copy in own:
        copy.wait()


GATHER_COPIES = 6 + 9 + 2 + 16 + 2 + 4


def gather_pages(page_cache, weights):
    rows = page_cache.shape[1]
    anywhere = pl.BlockSpec(memory_space=pl.ANY)
    return pl.pallas_call(
        gather_kernel,
        out_shape=(
            jax.ShapeDtypeStruct((2, 4, 4, 2, rows, HD), jnp.bfloat16),
            jax.ShapeDtypeStruct((4,) + weights.shape, jnp.bfloat16),
        ),
        in_specs=[anywhere, anywhere],
        out_specs=(anywhere, anywhere),
        scratch_shapes=[
            pltpu.SemaphoreType.DMA((2,)),
            pltpu.SemaphoreType.DMA((GATHER_COPIES,)),
            pltpu.SemaphoreType.DMA((GATHER_COPIES,)),
        ],
        compiler_params=pltpu.CompilerParams(collective_id=0, has_side_effects=True),
        name="gather_pages",
    )(page_cache, weights)


LANES = ((0, 256), (256, 256), (512, 256), (768, 128))
EXTRA = 16


def attention_kernel(
    slot_ref, parent_ref, count_ref, lost_ref, q_ref, new_ref, kv_ref, out_ref, keys, values, query, top, total
):
    pages_here = q_ref.shape[0] // PAGE
    scale = math.log2(math.e) / math.sqrt(HD)
    base = lax.axis_index("ctx") * pages_here
    token = lax.broadcasted_iota(jnp.int32, (16, HD), 0)
    nt = (((1,), (1,)), ((), ()))

    def transposed(block):
        return block.T[: HD + EXTRA]

    def one_lost(j, unused):
        rows = pl.ds(pl.multiple_of(j * PAGE, PAGE), PAGE)

        def append(state):
            page, filled = state
            count = count_ref[page]
            first = slot_ref[page] * PAGE
            at = pl.ds(pl.multiple_of(first, PAGE), PAGE)
            to = pl.ds(pl.multiple_of(filled, 16), PAGE)
            keys[to, :] = kv_ref[0, at, :]
            values[to, :HD] = kv_ref[1, at, :]
            values[to, HD:] = jnp.ones((PAGE, HD), jnp.bfloat16)
            last = ((count - 1) // 16) * 16
            kept = token + last < count
            at = pl.ds(pl.multiple_of(first + last, 16), 16)
            to = pl.ds(pl.multiple_of(filled + last, 16), 16)
            lead = kv_ref[0, pl.ds(pl.multiple_of(first, PAGE), 16), :].astype(jnp.float32)[:1, :]
            keys[to, :] = jnp.where(kept, kv_ref[0, at, :].astype(jnp.float32), lead).astype(jnp.bfloat16)
            values[to, :HD] = jnp.where(kept, kv_ref[1, at, :].astype(jnp.float32), 0.0).astype(jnp.bfloat16)
            values[to, HD:] = kept.astype(jnp.float32).astype(jnp.bfloat16)
            return parent_ref[page], filled + last + 16

        unused_page, filled = lax.while_loop(
            lambda state: state[0] >= 0, append, (lost_ref[base + j], jnp.int32(0))
        )
        tail = pl.ds(pl.multiple_of(filled, 16), CHUNK)
        lead = keys[:16, :].astype(jnp.float32)[:1, :]
        keys[tail, :] = jnp.broadcast_to(lead, (CHUNK, HD)).astype(jnp.bfloat16)
        values[tail, :] = jnp.zeros((CHUNK, 2 * HD), jnp.bfloat16)
        for h in range(GROUP):
            query[h * PAGE : (h + 1) * PAGE, :] = q_ref[rows, h * HD : (h + 1) * HD]

        with_ones = transposed(
            jnp.concatenate([new_ref[1, rows, :], jnp.ones((PAGE, HD), jnp.bfloat16)], axis=1)
        )
        for start, width in LANES:
            lanes = pl.ds(start, width)
            score = lax.dot_general(
                new_ref[0, rows, :], query[lanes, :], nt, preferred_element_type=jnp.float32
            )
            k_at = lax.broadcasted_iota(jnp.int32, (PAGE, width), 0)
            q_at = lax.broadcasted_iota(jnp.int32, (PAGE, width), 1) % PAGE
            seen = k_at <= q_at
            score = jnp.where(seen, score, -1e30)
            highest = jnp.max(score, axis=0, keepdims=True)
            weight = jnp.where(seen, jnp.exp2(score * scale - highest * scale), 0.0).astype(jnp.bfloat16)
            top[:, lanes] = jnp.broadcast_to(highest, (8, width))
            total[:, lanes] = jnp.dot(with_ones, weight, preferred_element_type=jnp.float32)

        def one_chunk(n, unused):
            at = pl.ds(pl.multiple_of(n * CHUNK, CHUNK), CHUNK)
            key = keys[at, :]
            value = transposed(values[at, :])
            for start, width in LANES:
                lanes = pl.ds(start, width)
                score = lax.dot_general(key, query[lanes, :], nt, preferred_element_type=jnp.float32)
                before = top[:1, lanes]
                highest = jnp.maximum(before, jnp.max(score, axis=0, keepdims=True))
                weight = jnp.exp2(score * scale - highest * scale).astype(jnp.bfloat16)
                factor = jnp.exp2((before - highest) * scale)
                top[:, lanes] = jnp.broadcast_to(highest, (8, width))
                total[:, lanes] = total[:, lanes] * factor + jnp.dot(
                    value, weight, preferred_element_type=jnp.float32
                )
            return unused

        lax.fori_loop(0, (filled + CHUNK - 1) // CHUNK, one_chunk, 0)
        for h in range(GROUP):
            lanes = pl.ds(h * PAGE, PAGE)
            out_ref[h * HD : (h + 1) * HD, rows] = (total[:HD, lanes] / total[HD : HD + 1, lanes]).astype(
                jnp.bfloat16
            )
        return unused

    lax.fori_loop(0, pages_here, one_lost, 0)


def attend(queries, new_kv, kv, page_slot, parent, valid_count, lost_parent):
    rows = kv.shape[1]
    smem = pl.BlockSpec(memory_space=pltpu.SMEM)
    vmem = pl.BlockSpec(memory_space=pltpu.VMEM)
    return pl.pallas_call(
        attention_kernel,
        out_shape=jax.ShapeDtypeStruct(queries.shape[::-1], jnp.bfloat16),
        in_specs=[smem] * 4 + [vmem] * 3,
        out_specs=vmem,
        scratch_shapes=[
            pltpu.VMEM((rows + CHUNK, HD), jnp.bfloat16),
            pltpu.VMEM((rows + CHUNK, 2 * HD), jnp.bfloat16),
            pltpu.VMEM((GROUP * PAGE, HD), jnp.bfloat16),
            pltpu.VMEM((8, GROUP * PAGE), jnp.float32),
            pltpu.VMEM((HD + EXTRA, GROUP * PAGE), jnp.float32),
        ],
        compiler_params=pltpu.CompilerParams(vmem_limit_bytes=VMEM_LIMIT),
        name="attend",
    )(page_slot, parent, valid_count, lost_parent, queries, new_kv, kv)


OWN = [(0, 0), (0, 1)]
NEAR = [(1, 0), (3, 0), (1, 1), (3, 1)]
FAR = [(2, 0), (2, 1)]
WAVES = []
for _w in range(6):
    for _delay, _blocks in ((0, OWN), (1, NEAR), (2, FAR)):
        if 0 <= _w - _delay < 4:
            WAVES += [(_block, _w - _delay) for _block in _blocks]


def project_kernel(
    att_ref, w_ref, out_ref, peers, outgoing, incoming, a_send, a_recv, z_send, z_recv, f_send, f_recv
):
    x, y, k, t = place()
    here = ctx_of(x, y, k)

    def holder(dy, dk):
        return (ctx_of(x, lax.rem(y + dy, 4), k if dk == 0 else 1 - k), t)

    columns = w_ref.shape[1]
    width = att_ref.shape[1] // 2
    sides = (pl.ds(0, width), pl.ds(width, width))
    mine = lax.rem(y, 2) * 2 + k
    late = lax.rem(t + lax.div(y, 2), 2)
    barrier = pltpu.get_barrier_semaphore()
    others = [(dy, dk) for dy in range(4) for dk in range(2) if (dy, dk) != (0, 0)]
    for device in [holder(dy, dk) for dy, dk in others] + [(here, lax.rem(t + 1, 8)), (here, lax.rem(t + 7, 8))]:
        pl.semaphore_signal(barrier, inc=1, device_id=device, device_id_type=MESH)
    pl.semaphore_wait(barrier, 9)

    a_copies = []

    def share(src, dst, device):
        n = len(a_copies)
        copy = pltpu.make_async_remote_copy(
            src, dst, a_send.at[n], a_recv.at[n], device_id=device, device_id_type=MESH
        )
        copy.start()
        a_copies.append(copy)
        return copy

    core = {0: share(att_ref, peers.at[0, 1], holder(0, 1))}
    near = {3: share(att_ref, peers.at[3, 0], holder(1, 0)), 1: share(att_ref, peers.at[1, 0], holder(3, 0))}
    far = {}

    def need(dy, dk):
        if (dy, dk) == (0, 0):
            return
        if dk == 1:
            core[dy].wait_recv()
        elif dy in near:
            near[dy].wait_recv()
            side = 0 if dy == 3 else 1
            far[side] = share(
                peers.at[dy, 0, :, sides[side]],
                peers.at[2, 0, :, sides[side]],
                holder(1 if dy == 3 else 3, 0),
            )
            core[dy] = share(peers.at[dy, 0], peers.at[dy, 1], holder(0, 1))
        else:
            far[0].wait_recv()
            far[1].wait_recv()
            core[2] = share(peers.at[2, 0], peers.at[2, 1], holder(0, 1))

    def hop(block, i, side):
        dy, dk = block
        step = (1 - 2 * k) * (1 - 2 * dk)
        slot = i + 1 - late
        return pltpu.make_async_remote_copy(
            outgoing.at[dy, dk, i, :, sides[side]],
            incoming.at[dy, dk, slot, :, sides[side]],
            z_send.at[dy, dk, i, side],
            z_recv.at[dy, dk, slot, side],
            device_id=(here, lax.rem(t + step + 8, 8)),
            device_id_type=MESH,
        )

    def arrived(block, i, side):
        dy, dk = block
        spot = incoming.at[dy, dk, i, :, sides[side]]
        pltpu.make_async_copy(spot, spot, z_recv.at[dy, dk, i, side]).wait()

    spot = pl.ds(pl.multiple_of(mine * columns, 16), columns)

    def result(block):
        dy, dk = block
        return pltpu.make_async_remote_copy(
            outgoing.at[dy, dk, 3],
            out_ref.at[spot, :],
            f_send.at[dy, dk],
            f_recv.at[mine],
            device_id=holder(dy, dk),
            device_id_type=MESH,
        )

    for block, i in WAVES:
        dy, dk = block
        if i == 0:
            need(dy, dk)
        step = (1 - 2 * k) * (1 - 2 * dk)
        target = lax.rem(t - step * (2 * i + 2 - late) + 16, 8)
        rows = att_ref[...] if block == (0, 0) else peers[dy, dk]
        term = jnp.dot(w_ref[lax.div(target, 2)], rows, preferred_element_type=jnp.float32)

        def add_and_send(block=block, i=i, term=term, send=True):
            dy, dk = block
            for side in (0, 1):
                arrived(block, i, side)
                cut = slice(side * width, (side + 1) * width)
                total = term[:, cut] + incoming[dy, dk, i, :, sides[side]].astype(jnp.float32)
                outgoing[dy, dk, i, :, sides[side]] = total.astype(jnp.bfloat16)
                if send:
                    hop(block, i, side).start()

        if i == 0:

            @pl.when(late == 1)
            def _(block=block, i=i, term=term):
                dy, dk = block
                outgoing[dy, dk, i] = term.astype(jnp.bfloat16)
                hop(block, i, 0).start()
                hop(block, i, 1).start()

            pl.when(late == 0)(add_and_send)
        elif i < 3:
            add_and_send()
        else:
            pl.when(late == 1)(add_and_send)

            @pl.when(late == 0)
            def _(block=block, i=i, term=term, add=add_and_send):
                dy, dk = block
                add(block, i, term, False)
                if block == (0, 0):
                    out_ref[spot, :] = outgoing[0, 0, 3]
                else:
                    result(block).start()

    for n in range(4):

        @pl.when((late == 1) | (mine != n))
        def _(n=n):
            landed = out_ref.at[pl.ds(n * columns, columns), :]
            pltpu.make_async_copy(landed, landed, f_recv.at[n]).wait()

    for copy in a_copies:
        copy.wait_send()
    for block in OWN + NEAR + FAR:
        for i in range(3):
            hop(block, i, 0).wait_send()
            hop(block, i, 1).wait_send()

        @pl.when(late == 1)
        def _(block=block):
            hop(block, 3, 0).wait_send()
            hop(block, 3, 1).wait_send()

        if block != (0, 0):

            @pl.when(late == 0)
            def _(block=block):
                result(block).wait_send()


def project(attended, weights):
    depth, rows = attended.shape
    columns = weights.shape[1]
    vmem = pl.BlockSpec(memory_space=pltpu.VMEM)
    return pl.pallas_call(
        project_kernel,
        out_shape=jax.ShapeDtypeStruct((4 * columns, rows), jnp.bfloat16),
        in_specs=[vmem, vmem],
        out_specs=vmem,
        scratch_shapes=[
            pltpu.VMEM((4, 2, depth, rows), jnp.bfloat16),
            pltpu.VMEM((4, 2, 4, columns, rows), jnp.bfloat16),
            pltpu.VMEM((4, 2, 4, columns, rows), jnp.bfloat16),
            pltpu.SemaphoreType.DMA((8,)),
            pltpu.SemaphoreType.DMA((8,)),
            pltpu.SemaphoreType.DMA((4, 2, 4, 2)),
            pltpu.SemaphoreType.DMA((4, 2, 4, 2)),
            pltpu.SemaphoreType.DMA((4, 2)),
            pltpu.SemaphoreType.DMA((4,)),
        ],
        compiler_params=pltpu.CompilerParams(
            collective_id=1, has_side_effects=True, vmem_limit_bytes=VMEM_LIMIT
        ),
        name="project",
    )(attended, weights)


def per_device(
    queries, new_kv, page_cache, out_weight, page_slot, parent, valid_count, lost_parent
):
    kv, weights = gather_pages(page_cache, out_weight.T)
    kv = kv.reshape(2, -1, HD)
    attended = attend(queries, new_kv, kv, page_slot, parent, valid_count, lost_parent)
    return project(attended, weights).T


def solution(mesh):
    return jax.shard_map(
        per_device,
        mesh=mesh,
        in_specs=(
            P("ctx", "tp"),
            P(None, "ctx", "tp"),
            P(None, "ctx", "tp"),
            P("tp", "ctx"),
            P(),
            P(),
            P(),
            P(),
        ),
        out_specs=P("ctx", "tp"),
        check_vma=False,
    )
```

time: 153 us -> 126 us (0.82); the launches traced: 150 us -> 125 us
  waiting for transfers between devices: 29.8 us -> 0 us
  between operations: 13.4 us -> 0.05 us
  Pallas kernels: 105 us -> 117 us
  local copies, waits for them, and re-layouts: 1.99 us -> 7.7 us
    all_gather x1 -> x0, waiting for transfers between devices: 29.1 us -> none  [per_device(): lax.all_gather(out_weight.T, 'ctx', axis_index_groups=weight_groups())]
    pallas_call x1, Pallas kernels: 59.2 us -> 72 us  [project(): pl.pallas_call(project_kernel, out_shape=jax.ShapeDtypeStruct((4 * column...]
    unnamed x0 -> x16, local copies, waits for them, and re-layouts: none -> 6.73 us
    pallas_call x1, Pallas kernels: 17 us -> 15.3 us  [attend(): pl.pallas_call(attention_kernel, out_shape=jax.ShapeDtypeStruct(queries.s...]
  transfers between devices with their start and end apart: 1 -> 0, of which waited for: 1 -> 0; matrix products, arithmetic and copies ran while one was open for 0% -> 0% of each run, Pallas kernels for 30% -> 0%
where the time goes in v2:
time: 126 us; the launch traced here: 125 us
  Pallas kernels  117 us (93%)
  local copies, waits for them, and re-layouts  7.7 us (6%)
    pallas_call x1, Pallas kernels, project(): pl.pallas_call(project_kernel, out_shape=jax.ShapeDtypeStruct((4 * column...  72 us
    pallas_call x1, Pallas kernels, gather_pages(): pl.pallas_call(gather_kernel, out_shape=(jax.ShapeDtypeStruct((2, 4, 4, 2...  29.6 us
    pallas_call x1, Pallas kernels, attend(): pl.pallas_call(attention_kernel, out_shape=jax.ShapeDtypeStruct(queries.s...  15.3 us
    unnamed x16, local copies, waits for them, and re-layouts  6.73 us

profile of v2, /device:TPU:33, one launch (start us, length us, event | category | flops | bytes accessed | tf_op | source)
XLA Modules:
  0.0 124.6 jit_solution(4610129376940180175)
XLA Ops:
  0.0 29.6 %gather_pages.1 = (bf16[2,4,4,2,256,128]{5,4,3,2,1,0:T(8,128)(2,1)}, bf16[4,224,896]{2,1,0:T(8,128)(2,1)}) custom-call(bf16[2,256,128]{2,1,0:T(8,128)(2,1)} %page_ref.1, bf16[224,896]{1,0:T(8,128)(2,1)} %bitcast.5), custom_call_target="tpu_custom_call" | custom-call | tf_op jit(solution)/shard_map/gather_pages/pallas_call | solution.py:121
  29.6 0.0 copy-start
  29.6 2.2 %copy-done = bf16[2,4,4,2,256,128]{5,4,3,2,1,0:T(8,128)(2,1)S(1)} copy-done((bf16[2,4,4,2,256,128]{5,4,3,2,1,0:T(8,128)(2,1)S(1)}, bf16[2,4,4,2,256,128]{5,4,3,2,1,0:T(8,128)(2,1)}, u32[]{:S(2)}) %copy-start) | copy-done | bytes 4194328
  31.8 0.0 copy-start.2
  31.8 1.0 copy-done.2
  32.8 0.0 copy-start.3
  32.8 0.9 copy-done.3
  33.7 0.0 copy-start.4
  33.7 0.7 copy-done.4
  34.4 0.0 copy-start.5
  34.4 0.7 copy-done.5
  35.0 0.0 copy-start.6
  35.0 0.7 copy-done.6
  35.7 0.0 copy-start.7
  35.7 0.7 copy-done.7
  36.3 0.0 copy-start.1
  36.3 15.3 %attend.1.att_ref = bf16[896,256]{1,0:T(8,128)(2,1)S(1)} custom-call(s32[64]{0:T(128)S(1)} %copy-done.4, s32[64]{0:T(128)S(1)} %copy-done.5, s32[64]{0:T(128)S(1)} %copy-done.6, s32[64]{0:T(128)S(1)} %copy-done.7, bf16[256,896]{1,0:T(8,128)(2,1)S(1)} %copy-done.2, bf16[2,256,128]{2,1,0:T(8,128)(2,1)S(1)} %copy-done.3, bf16[2,8192,128]{2,1,0:T(8,128)(2,1)S(1)} %bitcast.3), custom_call_target="tpu_custom_call" | custom-call | tf_op jit(solution)/shard_map/attend/pallas_call | solution.py:236
  51.6 0.0 copy-done.1
  51.6 72.0 %project.1 = bf16[896,256]{1,0:T(8,128)(2,1)S(1)} custom-call(bf16[896,256]{1,0:T(8,128)(2,1)S(1)} %attend.1.att_ref, bf16[4,224,896]{2,1,0:T(8,128)(2,1)S(1)} %copy-done.1), custom_call_target="tpu_custom_call" | custom-call | tf_op jit(solution)/shard_map/project/pallas_call | solution.py:421
  123.6 1.0 copy.9
Async XLA Ops:
  29.6 2.2 %copy-start = (bf16[2,4,4,2,256,128]{5,4,3,2,1,0:T(8,128)(2,1)S(1)}, bf16[2,4,4,2,256,128]{5,4,3,2,1,0:T(8,128)(2,1)}, u32[]{:S(2)}) copy-start(bf16[2,4,4,2,256,128]{5,4,3,2,1,0:T(8,128)(2,1)} %get-tuple-element.7) | copy-start | bytes 12582916
  31.8 1.0 copy-start.2
  32.8 0.9 copy-start.3
  33.7 0.7 copy-start.4
  34.4 0.7 copy-start.5
  35.0 0.7 copy-start.6
  35.7 0.7 copy-start.7
  36.3 15.3 %copy-start.1 = (bf16[4,224,896]{2,1,0:T(8,128)(2,1)S(1)}, bf16[4,224,896]{2,1,0:T(8,128)(2,1)}, u32[]{:S(2)}) copy-start(bf16[4,224,896]{2,1,0:T(8,128)(2,1)} %get-tuple-element.8.w_ref) | copy-start | bytes 4816900

commit v3 on v2

--- a/solution.py
+++ b/solution.py
@@ -12,9 +12,9 @@
 HD = 128
 PAGE = 128
 GROUP = HEADS // KV_HEADS
-CHUNK = 512
+CHUNK = 768
 MESH = pl.DeviceIdType.MESH
-VMEM_LIMIT = 28 * 2**20
+VMEM_LIMIT = 56 * 2**20
 
 
 def place():
@@ -136,7 +136,7 @@
     )(page_cache, weights)
 
 
-LANES = ((0, 256), (256, 256), (512, 256), (768, 128))
+LANES = ((0, GROUP * PAGE),)
 EXTRA = 16
 
 
@@ -261,7 +261,7 @@
 
 
 def project_kernel(
-    att_ref, w_ref, out_ref, peers, outgoing, incoming, a_send, a_recv, z_send, z_recv, f_send, f_recv
+    att_ref, w_ref, out_ref, peers, terms, outgoing, incoming, a_send, a_recv, z_send, z_recv, f_send, f_recv
 ):
     x, y, k, t = place()
     here = ctx_of(x, y, k)
@@ -269,7 +269,7 @@
     def holder(dy, dk):
         return (ctx_of(x, lax.rem(y + dy, 4), k if dk == 0 else 1 - k), t)
 
-    columns = w_ref.shape[1]
+    columns = w_ref.shape[0] // 4
     width = att_ref.shape[1] // 2
     sides = (pl.ds(0, width), pl.ds(width, width))
     mine = lax.rem(y, 2) * 2 + k
@@ -319,8 +319,8 @@
         step = (1 - 2 * k) * (1 - 2 * dk)
         slot = i + 1 - late
         return pltpu.make_async_remote_copy(
-            outgoing.at[dy, dk, i, :, sides[side]],
-            incoming.at[dy, dk, slot, :, sides[side]],
+            outgoing.at[dy, dk, i, side],
+            incoming.at[dy, dk, slot, side],
             z_send.at[dy, dk, i, side],
             z_recv.at[dy, dk, slot, side],
             device_id=(here, lax.rem(t + step + 8, 8)),
@@ -329,71 +329,75 @@
 
     def arrived(block, i, side):
         dy, dk = block
-        spot = incoming.at[dy, dk, i, :, sides[side]]
+        spot = incoming.at[dy, dk, i, side]
         pltpu.make_async_copy(spot, spot, z_recv.at[dy, dk, i, side]).wait()
 
     spot = pl.ds(pl.multiple_of(mine * columns, 16), columns)
 
-    def result(block):
+    def result(block, side):
         dy, dk = block
         return pltpu.make_async_remote_copy(
-            outgoing.at[dy, dk, 3],
-            out_ref.at[spot, :],
-            f_send.at[dy, dk],
-            f_recv.at[mine],
+            outgoing.at[dy, dk, 3, side],
+            out_ref.at[spot, sides[side]],
+            f_send.at[dy, dk, side],
+            f_recv.at[mine, side],
             device_id=holder(dy, dk),
             device_id_type=MESH,
         )
 
+    def add(block, i, side):
+        dy, dk = block
+        step = (1 - 2 * k) * (1 - 2 * dk)
+        target = lax.rem(t - step * (2 * i + 2 - late) + 16, 8)
+        at = pl.ds(pl.multiple_of(lax.div(target, 2) * columns, 32), columns)
+        return terms[dy, dk, at, side * width : (side + 1) * width]
+
+    def first(block, i):
+        dy, dk = block
+        for side in (0, 1):
+            outgoing[dy, dk, i, side] = add(block, i, side).astype(jnp.bfloat16)
+            hop(block, i, side).start()
+
+    def pass_on(block, i):
+        dy, dk = block
+        for side in (0, 1):
+            arrived(block, i, side)
+            total = add(block, i, side) + incoming[dy, dk, i, side].astype(jnp.float32)
+            outgoing[dy, dk, i, side] = total.astype(jnp.bfloat16)
+            hop(block, i, side).start()
+
+    def finish(block, i):
+        dy, dk = block
+        for side in (0, 1):
+            arrived(block, i, side)
+            total = add(block, i, side) + incoming[dy, dk, i, side].astype(jnp.float32)
+            if block == (0, 0):
+                out_ref[spot, sides[side]] = total.astype(jnp.bfloat16)
+            else:
+                outgoing[dy, dk, i, side] = total.astype(jnp.bfloat16)
+                result(block, side).start()
+
     for block, i in WAVES:
         dy, dk = block
         if i == 0:
             need(dy, dk)
-        step = (1 - 2 * k) * (1 - 2 * dk)
-        target = lax.rem(t - step * (2 * i + 2 - late) + 16, 8)
-        rows = att_ref[...] if block == (0, 0) else peers[dy, dk]
-        term = jnp.dot(w_ref[lax.div(target, 2)], rows, preferred_element_type=jnp.float32)
-
-        def add_and_send(block=block, i=i, term=term, send=True):
-            dy, dk = block
-            for side in (0, 1):
-                arrived(block, i, side)
-                cut = slice(side * width, (side + 1) * width)
-                total = term[:, cut] + incoming[dy, dk, i, :, sides[side]].astype(jnp.float32)
-                outgoing[dy, dk, i, :, sides[side]] = total.astype(jnp.bfloat16)
-                if send:
-                    hop(block, i, side).start()
-
-        if i == 0:
-
-            @pl.when(late == 1)
-            def _(block=block, i=i, term=term):
-                dy, dk = block
-                outgoing[dy, dk, i] = term.astype(jnp.bfloat16)
-                hop(block, i, 0).start()
-                hop(block, i, 1).start()
-
-            pl.when(late == 0)(add_and_send)
+            rows = att_ref[...] if block == (0, 0) else peers[dy, dk]
+            terms[dy, dk] = jnp.dot(w_ref[...], rows, preferred_element_type=jnp.float32)
+            pl.when(late == 1)(lambda block=block: first(block, 0))
+            pl.when(late == 0)(lambda block=block: pass_on(block, 0))
         elif i < 3:
-            add_and_send()
+            pass_on(block, i)
         else:
-            pl.when(late == 1)(add_and_send)
-
-            @pl.when(late == 0)
-            def _(block=block, i=i, term=term, add=add_and_send):
-                dy, dk = block
-                add(block, i, term, False)
-                if block == (0, 0):
-                    out_ref[spot, :] = outgoing[0, 0, 3]
-                else:
-                    result(block).start()
+            pl.when(late == 1)(lambda block=block: pass_on(block, 3))
+            pl.when(late == 0)(lambda block=block: finish(block, 3))
 
     for n in range(4):
 
         @pl.when((late == 1) | (mine != n))
         def _(n=n):
-            landed = out_ref.at[pl.ds(n * columns, columns), :]
-            pltpu.make_async_copy(landed, landed, f_recv.at[n]).wait()
+            for side in (0, 1):
+                landed = out_ref.at[pl.ds(n * columns, columns), sides[side]]
+                pltpu.make_async_copy(landed, landed, f_recv.at[n, side]).wait()
 
     for copy in a_copies:
         copy.wait_send()
@@ -411,12 +415,13 @@
 
             @pl.when(late == 0)
             def _(block=block):
-                result(block).wait_send()
+                result(block, 0).wait_send()
+                result(block, 1).wait_send()
 
 
 def project(attended, weights):
     depth, rows = attended.shape
-    columns = weights.shape[1]
+    columns = weights.shape[0] // 4
     vmem = pl.BlockSpec(memory_space=pltpu.VMEM)
     return pl.pallas_call(
         project_kernel,
@@ -425,14 +430,15 @@
         out_specs=vmem,
         scratch_shapes=[
             pltpu.VMEM((4, 2, depth, rows), jnp.bfloat16),
-            pltpu.VMEM((4, 2, 4, columns, rows), jnp.bfloat16),
-            pltpu.VMEM((4, 2, 4, columns, rows), jnp.bfloat16),
+            pltpu.VMEM((4, 2, 4 * columns, rows), jnp.float32),
+            pltpu.VMEM((4, 2, 4, 2, columns, rows // 2), jnp.bfloat16),
+            pltpu.VMEM((4, 2, 4, 2, columns, rows // 2), jnp.bfloat16),
             pltpu.SemaphoreType.DMA((8,)),
             pltpu.SemaphoreType.DMA((8,)),
             pltpu.SemaphoreType.DMA((4, 2, 4, 2)),
             pltpu.SemaphoreType.DMA((4, 2, 4, 2)),
+            pltpu.SemaphoreType.DMA((4, 2, 2)),
             pltpu.SemaphoreType.DMA((4, 2)),
-            pltpu.SemaphoreType.DMA((4,)),
         ],
         compiler_params=pltpu.CompilerParams(
             collective_id=1, has_side_effects=True, vmem_limit_bytes=VMEM_LIMIT
@@ -447,7 +453,7 @@
     kv, weights = gather_pages(page_cache, out_weight.T)
     kv = kv.reshape(2, -1, HD)
     attended = attend(queries, new_kv, kv, page_slot, parent, valid_count, lost_parent)
-    return project(attended, weights).T
+    return project(attended, weights.reshape(-1, weights.shape[2])).T
 
 
 def solution(mesh):

time: 126 us -> 121 us (0.960)
  local copies, waits for them, and re-layouts: 7.7 us -> 1.99 us
    unnamed x16 -> x0, local copies, waits for them, and re-layouts: 6.73 us -> none
where the time goes in v3:
time: 121 us; the launch traced here: 119 us
  Pallas kernels  117 us (97%)
  local copies, waits for them, and re-layouts  1.99 us (2%)
    pallas_call x1, Pallas kernels, project(): pl.pallas_call(project_kernel, out_shape=jax.ShapeDtypeStruct((4 * column...  72.1 us
    pallas_call x1, Pallas kernels, gather_pages(): pl.pallas_call(gather_kernel, out_shape=(jax.ShapeDtypeStruct((2, 4, 4, 2...  29.6 us
    pallas_call x1, Pallas kernels, attend(): pl.pallas_call(attention_kernel, out_shape=jax.ShapeDtypeStruct(queries.s...  15.6 us

profile of v3, /device:TPU:33, one launch (start us, length us, event | category | flops | bytes accessed | tf_op | source)
XLA Modules:
  0.0 119.4 jit_solution(17068174764000883460)
XLA Ops:
  0.0 29.6 %gather_pages.1 = (bf16[2,4,4,2,256,128]{5,4,3,2,1,0:T(8,128)(2,1)}, bf16[4,224,896]{2,1,0:T(8,128)(2,1)}) custom-call(bf16[2,256,128]{2,1,0:T(8,128)(2,1)} %page_ref.1, bf16[224,896]{1,0:T(8,128)(2,1)} %bitcast.7), custom_call_target="tpu_custom_call" | custom-call | tf_op jit(solution)/shard_map/gather_pages/pallas_call | solution.py:121
  29.6 15.6 %attend.1.att_ref = bf16[896,256]{1,0:T(8,128)(2,1)} custom-call(s32[64]{0:T(128)} %slot_ref.1, s32[64]{0:T(128)} %parent_ref.1, s32[64]{0:T(128)} %count_ref.1, s32[64]{0:T(128)} %lost_ref.1, bf16[256,896]{1,0:T(8,128)(2,1)} %q_ref.1, bf16[2,256,128]{2,1,0:T(8,128)(2,1)} %new_ref.1, bf16[2,8192,128]{2,1,0:T(8,128)(2,1)} %bitcast.4), custom_call_target="tpu_custom_call" | custom-call | tf_op jit(solution)/shard_map/attend/pallas_call | solution.py:236
  45.2 72.1 %project.1 = bf16[896,256]{1,0:T(8,128)(2,1)} custom-call(bf16[896,256]{1,0:T(8,128)(2,1)} %attend.1.att_ref, bf16[896,896]{1,0:T(8,128)(2,1)} %bitcast.6), custom_call_target="tpu_custom_call" | custom-call | tf_op jit(solution)/shard_map/project/pallas_call | solution.py:426
  117.4 2.0 %copy.9 = bf16[256,896]{1,0:T(8,128)(2,1)} copy(bf16[256,896]{0,1:T(8,128)(2,1)} %bitcast.5) | data formatting | bytes 917504 | tf_op jit(solution)/shard_map/transpose | solution.py:456

commit v4 on v3

--- a/solution.py
+++ b/solution.py
@@ -37,15 +37,13 @@
 
     other = (ctx_of(x, y, 1 - k), t)
     barrier = pltpu.get_barrier_semaphore()
-    for device in (at_x(1), at_x(2), at_x(3), at_y(1), at_y(3), other):
+    for device in (at_x(1), at_x(2), at_x(3), at_y(1), at_y(2), at_y(3), other):
         pl.semaphore_signal(barrier, inc=1, device_id=device, device_id_type=MESH)
-    own = [
-        pltpu.make_async_copy(page_ref, kv_ref.at[:, x, y, k], own_sem.at[0]),
-        pltpu.make_async_copy(w_ref, wall_ref.at[x], own_sem.at[1]),
-    ]
-    for copy in own:
-        copy.start()
-    pl.semaphore_wait(barrier, 6)
+    own = pltpu.make_async_copy(page_ref, kv_ref.at[:, x, y, k], own_sem.at[0])
+    own.start()
+    kept = pltpu.make_async_copy(w_ref, wall_ref.at[x], own_sem.at[1])
+    pl.when(k == 0)(kept.start)
+    pl.semaphore_wait(barrier, 7)
 
     copies = []
 
@@ -64,10 +62,14 @@
     def half(part, dx, dy):
         return kv_ref.at[part, lax.rem(x + dx, 4), lax.rem(y + dy, 4), k]
 
+    swapped = pltpu.make_async_remote_copy(
+        w_ref, wall_ref.at[x], own_sem.at[2], own_sem.at[3], device_id=at_y(2), device_id_type=MESH
+    )
     home = piece(0, 0)
     along = {d: remote(page_ref, home, at_x(d)) for d in (1, 3, 2)}
     up = {0: remote(page_ref, home, at_y(1))}
     down = {0: remote(page_ref, home, at_y(3))}
+    pl.when(k == 1)(swapped.start)
     shared = [remote(page_ref, home, other)]
     for d in (1, 3, 2):
         along[d].wait_recv()
@@ -75,8 +77,10 @@
         up[d] = remote(here, here, at_y(1))
         down[d] = remote(here, here, at_y(3))
         shared.append(remote(here, here, other))
-    right = remote(w_ref, wall_ref.at[x], at_x(1))
-    left = remote(w_ref, wall_ref.at[x], at_x(3))
+    pl.when(k == 0)(kept.wait)
+    pl.when(k == 1)(swapped.wait_recv)
+    right = remote(wall_ref.at[x], wall_ref.at[x], at_x(1))
+    left = remote(wall_ref.at[x], wall_ref.at[x], at_x(3))
     far = {}
     far_w = []
     middle = w_ref.shape[0] // 2
@@ -108,8 +112,8 @@
         copy.wait_recv()
     for copy in copies:
         copy.wait_send()
-    for copy in own:
-        copy.wait()
+    pl.when(k == 1)(swapped.wait_send)
+    own.wait()
 
 
 GATHER_COPIES = 6 + 9 + 2 + 16 + 2 + 4
@@ -127,7 +131,7 @@
         in_specs=[anywhere, anywhere],
         out_specs=(anywhere, anywhere),
         scratch_shapes=[
-            pltpu.SemaphoreType.DMA((2,)),
+            pltpu.SemaphoreType.DMA((4,)),
             pltpu.SemaphoreType.DMA((GATHER_COPIES,)),
             pltpu.SemaphoreType.DMA((GATHER_COPIES,)),
         ],
@@ -250,14 +254,20 @@
     )(page_slot, parent, valid_count, lost_parent, queries, new_kv, kv)
 
 
-OWN = [(0, 0), (0, 1)]
-NEAR = [(1, 0), (3, 0), (1, 1), (3, 1)]
-FAR = [(2, 0), (2, 1)]
-WAVES = []
-for _w in range(6):
-    for _delay, _blocks in ((0, OWN), (1, NEAR), (2, FAR)):
-        if 0 <= _w - _delay < 4:
-            WAVES += [(_block, _w - _delay) for _block in _blocks]
+PARTS = [((0, 0), (0, 1), 0), ((0, 1), (0, 1), 0)]
+PARTS += [((dy, dk), (0,), 2) for dy in (1, 3) for dk in (0, 1)]
+PARTS += [((dy, dk), (1,), 3) for dy in (1, 3) for dk in (0, 1)]
+PARTS += [((2, dk), (0,), 3) for dk in (0, 1)]
+PARTS += [((2, dk), (1,), 4) for dk in (0, 1)]
+STEPS = 5
+WAVES = [
+    (block, sides, wave - delay)
+    for wave in range(STEPS + 4)
+    for block, sides, delay in PARTS
+    if 0 <= wave - delay < STEPS
+]
+EVEN = ((4, None, 0), (-2, 2, 2), (2, 0, 1))
+ODD = ((-3, None, 2), (3, 0, 0), (-1, 2, 3), (1, 1, 1))
 
 
 def project_kernel(
@@ -271,53 +281,49 @@
 
     columns = w_ref.shape[0] // 4
     width = att_ref.shape[1] // 2
-    sides = (pl.ds(0, width), pl.ds(width, width))
+    lanes = (pl.ds(0, width), pl.ds(width, width))
     mine = lax.rem(y, 2) * 2 + k
-    late = lax.rem(t + lax.div(y, 2), 2)
+    odd = lax.rem(t + lax.div(y, 2) + k, 2)
     barrier = pltpu.get_barrier_semaphore()
     others = [(dy, dk) for dy in range(4) for dk in range(2) if (dy, dk) != (0, 0)]
     for device in [holder(dy, dk) for dy, dk in others] + [(here, lax.rem(t + 1, 8)), (here, lax.rem(t + 7, 8))]:
         pl.semaphore_signal(barrier, inc=1, device_id=device, device_id_type=MESH)
     pl.semaphore_wait(barrier, 9)
 
-    a_copies = []
-
-    def share(src, dst, device):
-        n = len(a_copies)
+    def share(src, dy, dk, side, device):
         copy = pltpu.make_async_remote_copy(
-            src, dst, a_send.at[n], a_recv.at[n], device_id=device, device_id_type=MESH
+            src,
+            peers.at[dy, dk, side],
+            a_send.at[dy, dk, side],
+            a_recv.at[dy, dk, side],
+            device_id=device,
+            device_id_type=MESH,
         )
         copy.start()
-        a_copies.append(copy)
         return copy
 
-    core = {0: share(att_ref, peers.at[0, 1], holder(0, 1))}
-    near = {3: share(att_ref, peers.at[3, 0], holder(1, 0)), 1: share(att_ref, peers.at[1, 0], holder(3, 0))}
-    far = {}
-
-    def need(dy, dk):
+    shared = {}
+    for side in (0, 1):
+        mine_here = att_ref.at[:, lanes[side]]
+        shared[3, 0, side] = share(mine_here, 3, 0, side, holder(1, 0))
+        shared[1, 0, side] = share(mine_here, 1, 0, side, holder(3, 0))
+        shared[0, 1, side] = share(mine_here, 0, 1, side, holder(0, 1))
+
+    def need(dy, dk, side):
         if (dy, dk) == (0, 0):
             return
-        if dk == 1:
-            core[dy].wait_recv()
-        elif dy in near:
-            near[dy].wait_recv()
-            side = 0 if dy == 3 else 1
-            far[side] = share(
-                peers.at[dy, 0, :, sides[side]],
-                peers.at[2, 0, :, sides[side]],
-                holder(1 if dy == 3 else 3, 0),
-            )
-            core[dy] = share(peers.at[dy, 0], peers.at[dy, 1], holder(0, 1))
-        else:
-            far[0].wait_recv()
-            far[1].wait_recv()
-            core[2] = share(peers.at[2, 0], peers.at[2, 1], holder(0, 1))
-
-    def hop(block, i, side):
-        dy, dk = block
-        step = (1 - 2 * k) * (1 - 2 * dk)
-        slot = i + 1 - late
+        shared[dy, dk, side].wait_recv()
+        if dk == 0:
+            if dy == (3 if side == 0 else 1):
+                shared[2, 0, side] = share(peers.at[dy, 0, side], 2, 0, side, holder(4 - dy, 0))
+            shared[dy, 1, side] = share(peers.at[dy, 0, side], dy, 1, side, holder(0, 1))
+
+    def long_way(dk):
+        return (1 - 2 * k) * (1 - 2 * dk)
+
+    def hop(block, i, side, arm, slot):
+        dy, dk = block
+        step = long_way(dk) if arm > 0 else -long_way(dk)
         return pltpu.make_async_remote_copy(
             outgoing.at[dy, dk, i, side],
             incoming.at[dy, dk, slot, side],
@@ -327,10 +333,11 @@
             device_id_type=MESH,
         )
 
-    def arrived(block, i, side):
-        dy, dk = block
-        spot = incoming.at[dy, dk, i, side]
-        pltpu.make_async_copy(spot, spot, z_recv.at[dy, dk, i, side]).wait()
+    def arrived(block, slot, side):
+        dy, dk = block
+        spot = incoming.at[dy, dk, slot, side]
+        pltpu.make_async_copy(spot, spot, z_recv.at[dy, dk, slot, side]).wait()
+        return incoming[dy, dk, slot, side].astype(jnp.float32)
 
     spot = pl.ds(pl.multiple_of(mine * columns, 16), columns)
 
@@ -338,83 +345,84 @@
         dy, dk = block
         return pltpu.make_async_remote_copy(
             outgoing.at[dy, dk, 3, side],
-            out_ref.at[spot, sides[side]],
+            out_ref.at[spot, lanes[side]],
             f_send.at[dy, dk, side],
             f_recv.at[mine, side],
             device_id=holder(dy, dk),
             device_id_type=MESH,
         )
 
-    def add(block, i, side):
-        dy, dk = block
-        step = (1 - 2 * k) * (1 - 2 * dk)
-        target = lax.rem(t - step * (2 * i + 2 - late) + 16, 8)
+    def term(block, distance, side):
+        dy, dk = block
+        target = lax.rem(t + long_way(dk) * distance + 8, 8)
         at = pl.ds(pl.multiple_of(lax.div(target, 2) * columns, 32), columns)
         return terms[dy, dk, at, side * width : (side + 1) * width]
 
-    def first(block, i):
-        dy, dk = block
-        for side in (0, 1):
-            outgoing[dy, dk, i, side] = add(block, i, side).astype(jnp.bfloat16)
-            hop(block, i, side).start()
-
-    def pass_on(block, i):
-        dy, dk = block
-        for side in (0, 1):
-            arrived(block, i, side)
-            total = add(block, i, side) + incoming[dy, dk, i, side].astype(jnp.float32)
+    def pass_on(block, sides, i, table):
+        dy, dk = block
+        distance, source, slot = table[i]
+        for side in sides:
+            total = term(block, distance, side)
+            if source is not None:
+                total = total + arrived(block, source, side)
             outgoing[dy, dk, i, side] = total.astype(jnp.bfloat16)
-            hop(block, i, side).start()
-
-    def finish(block, i):
-        dy, dk = block
-        for side in (0, 1):
-            arrived(block, i, side)
-            total = add(block, i, side) + incoming[dy, dk, i, side].astype(jnp.float32)
+            hop(block, i, side, distance, slot).start()
+
+    def finish(block, sides):
+        dy, dk = block
+        for side in sides:
+            total = term(block, 0, side) + arrived(block, 3, side) + arrived(block, 1, side)
             if block == (0, 0):
-                out_ref[spot, sides[side]] = total.astype(jnp.bfloat16)
+                out_ref[spot, lanes[side]] = total.astype(jnp.bfloat16)
             else:
-                outgoing[dy, dk, i, side] = total.astype(jnp.bfloat16)
+                outgoing[dy, dk, 3, side] = total.astype(jnp.bfloat16)
                 result(block, side).start()
 
-    for block, i in WAVES:
+    for block, sides, i in WAVES:
         dy, dk = block
         if i == 0:
-            need(dy, dk)
-            rows = att_ref[...] if block == (0, 0) else peers[dy, dk]
-            terms[dy, dk] = jnp.dot(w_ref[...], rows, preferred_element_type=jnp.float32)
-            pl.when(late == 1)(lambda block=block: first(block, 0))
-            pl.when(late == 0)(lambda block=block: pass_on(block, 0))
-        elif i < 3:
-            pass_on(block, i)
-        else:
-            pl.when(late == 1)(lambda block=block: pass_on(block, 3))
-            pl.when(late == 0)(lambda block=block: finish(block, 3))
+            for side in sides:
+                need(dy, dk, side)
+            if block == (0, 0):
+                rows = att_ref[...]
+            elif len(sides) == 2:
+                rows = jnp.concatenate([peers[dy, dk, 0], peers[dy, dk, 1]], axis=1)
+            else:
+                rows = peers[dy, dk, sides[0]]
+            start = sides[0] * width
+            terms[dy, dk, :, start : start + len(sides) * width] = jnp.dot(
+                w_ref[...], rows, preferred_element_type=jnp.float32
+            )
+        if i < 4:
+            pl.when(odd == 1)(lambda block=block, sides=sides, i=i: pass_on(block, sides, i, ODD))
+        if i < 3:
+            pl.when(odd == 0)(lambda block=block, sides=sides, i=i: pass_on(block, sides, i, EVEN))
+        if i == 4:
+            pl.when(odd == 0)(lambda block=block, sides=sides: finish(block, sides))
 
     for n in range(4):
 
-        @pl.when((late == 1) | (mine != n))
+        @pl.when((odd == 1) | (mine != n))
         def _(n=n):
             for side in (0, 1):
-                landed = out_ref.at[pl.ds(n * columns, columns), sides[side]]
+                landed = out_ref.at[pl.ds(n * columns, columns), lanes[side]]
                 pltpu.make_async_copy(landed, landed, f_recv.at[n, side]).wait()
 
-    for copy in a_copies:
+    for copy in shared.values():
         copy.wait_send()
-    for block in OWN + NEAR + FAR:
-        for i in range(3):
-            hop(block, i, 0).wait_send()
-            hop(block, i, 1).wait_send()
-
-        @pl.when(late == 1)
+
+    def drain(block, table):
+        for i, (distance, source, slot) in enumerate(table):
+            for side in (0, 1):
+                hop(block, i, side, distance, slot).wait_send()
+
+    for block in [(0, 0)] + others:
+        pl.when(odd == 1)(lambda block=block: drain(block, ODD))
+
+        @pl.when(odd == 0)
         def _(block=block):
-            hop(block, 3, 0).wait_send()
-            hop(block, 3, 1).wait_send()
-
-        if block != (0, 0):
-
-            @pl.when(late == 0)
-            def _(block=block):
+            drain(block, EVEN)
+            if block != (0, 0):
                 result(block, 0).wait_send()
                 result(block, 1).wait_send()
 
@@ -429,12 +437,12 @@
         in_specs=[vmem, vmem],
         out_specs=vmem,
         scratch_shapes=[
-            pltpu.VMEM((4, 2, depth, rows), jnp.bfloat16),
+            pltpu.VMEM((4, 2, 2, depth, rows // 2), jnp.bfloat16),
             pltpu.VMEM((4, 2, 4 * columns, rows), jnp.float32),
             pltpu.VMEM((4, 2, 4, 2, columns, rows // 2), jnp.bfloat16),
             pltpu.VMEM((4, 2, 4, 2, columns, rows // 2), jnp.bfloat16),
-            pltpu.SemaphoreType.DMA((8,)),
-            pltpu.SemaphoreType.DMA((8,)),
+            pltpu.SemaphoreType.DMA((4, 2, 2)),
+            pltpu.SemaphoreType.DMA((4, 2, 2)),
             pltpu.SemaphoreType.DMA((4, 2, 4, 2)),
             pltpu.SemaphoreType.DMA((4, 2, 4, 2)),
             pltpu.SemaphoreType.DMA((4, 2, 2)),

time: 121 us -> 116 us (0.959); the launches traced: 119 us -> 116 us
  Pallas kernels: 117 us -> 114 us
    pallas_call x1, Pallas kernels: 72.1 us -> 63.2 us  [project(): pl.pallas_call(project_kernel, out_shape=jax.ShapeDtypeStruct((4 * column...]
    pallas_call x1, Pallas kernels: 29.6 us -> 36.5 us  [gather_pages(): pl.pallas_call(gather_kernel, out_shape=(jax.ShapeDtypeStruct((2, 4, 4, 2...]
    pallas_call x1, Pallas kernels: 15.6 us -> 14.2 us  [attend(): pl.pallas_call(attention_kernel, out_shape=jax.ShapeDtypeStruct(queries.s...]
where the time goes in v4:
time: 116 us
  Pallas kernels  114 us (98%)
  local copies, waits for them, and re-layouts  1.99 us (2%)
    pallas_call x1, Pallas kernels, project(): pl.pallas_call(project_kernel, out_shape=jax.ShapeDtypeStruct((4 * column...  63.2 us
    pallas_call x1, Pallas kernels, gather_pages(): pl.pallas_call(gather_kernel, out_shape=(jax.ShapeDtypeStruct((2, 4, 4, 2...  36.5 us
    pallas_call x1, Pallas kernels, attend(): pl.pallas_call(attention_kernel, out_shape=jax.ShapeDtypeStruct(queries.s...  14.2 us

profile of v4, /device:TPU:33, one launch (start us, length us, event | category | flops | bytes accessed | tf_op | source)
XLA Modules:
  0.0 115.9 jit_solution(8176955033521534396)
XLA Ops:
  0.0 36.5 %gather_pages.1 = (bf16[2,4,4,2,256,128]{5,4,3,2,1,0:T(8,128)(2,1)}, bf16[4,224,896]{2,1,0:T(8,128)(2,1)}) custom-call(bf16[2,256,128]{2,1,0:T(8,128)(2,1)} %page_ref.1, bf16[224,896]{1,0:T(8,128)(2,1)} %bitcast.7), custom_call_target="tpu_custom_call" | custom-call | tf_op jit(solution)/shard_map/gather_pages/pallas_call | solution.py:125
  36.5 14.2 %attend.1.att_ref = bf16[896,256]{1,0:T(8,128)(2,1)} custom-call(s32[64]{0:T(128)} %slot_ref.1, s32[64]{0:T(128)} %parent_ref.1, s32[64]{0:T(128)} %count_ref.1, s32[64]{0:T(128)} %lost_ref.1, bf16[256,896]{1,0:T(8,128)(2,1)} %q_ref.1, bf16[2,256,128]{2,1,0:T(8,128)(2,1)} %new_ref.1, bf16[2,8192,128]{2,1,0:T(8,128)(2,1)} %bitcast.4), custom_call_target="tpu_custom_call" | custom-call | tf_op jit(solution)/shard_map/attend/pallas_call | solution.py:240
  50.7 63.2 %project.1 = bf16[896,256]{1,0:T(8,128)(2,1)} custom-call(bf16[896,256]{1,0:T(8,128)(2,1)} %attend.1.att_ref, bf16[896,896]{1,0:T(8,128)(2,1)} %bitcast.6), custom_call_target="tpu_custom_call" | custom-call | tf_op jit(solution)/shard_map/project/pallas_call | solution.py:434
  113.9 2.0 %copy.9 = bf16[256,896]{1,0:T(8,128)(2,1)} copy(bf16[256,896]{0,1:T(8,128)(2,1)} %bitcast.5) | data formatting | bytes 917504 | tf_op jit(solution)/shard_map/transpose | solution.py:464

commit v5 on v4

--- a/solution.py
+++ b/solution.py
@@ -12,7 +12,7 @@
 HD = 128
 PAGE = 128
 GROUP = HEADS // KV_HEADS
-CHUNK = 768
+CHUNK = 512
 MESH = pl.DeviceIdType.MESH
 VMEM_LIMIT = 56 * 2**20
 
@@ -47,12 +47,20 @@
 
     copies = []
 
-    def remote(src, dst, device):
+    def remote(src, dst, device, odd_src=None):
         n = len(copies)
-        copy = pltpu.make_async_remote_copy(
-            src, dst, send_sem.at[n], recv_sem.at[n], device_id=device, device_id_type=MESH
-        )
-        copy.start()
+
+        def copy_from(ref):
+            return pltpu.make_async_remote_copy(
+                ref, dst, send_sem.at[n], recv_sem.at[n], device_id=device, device_id_type=MESH
+            )
+
+        copy = copy_from(src)
+        if odd_src is None:
+            copy.start()
+        else:
+            pl.when(k == 0)(copy.start)
+            pl.when(k == 1)(copy_from(odd_src).start)
         copies.append(copy)
         return copy
 
@@ -62,14 +70,25 @@
     def half(part, dx, dy):
         return kv_ref.at[part, lax.rem(x + dx, 4), lax.rem(y + dy, 4), k]
 
-    swapped = pltpu.make_async_remote_copy(
-        w_ref, wall_ref.at[x], own_sem.at[2], own_sem.at[3], device_id=at_y(2), device_id_type=MESH
-    )
+    middle = w_ref.shape[0] // 2
+    halves = (pl.ds(0, middle), pl.ds(middle, middle))
+    swapped = [
+        pltpu.make_async_remote_copy(
+            w_ref.at[halves[n]],
+            wall_ref.at[x, halves[n]],
+            own_sem.at[2 + n],
+            own_sem.at[4 + n],
+            device_id=(ctx_of(x, 3 - y, k), t),
+            device_id_type=MESH,
+        )
+        for n in (0, 1)
+    ]
+    for copy in swapped:
+        pl.when(k == 1)(copy.start)
     home = piece(0, 0)
     along = {d: remote(page_ref, home, at_x(d)) for d in (1, 3, 2)}
     up = {0: remote(page_ref, home, at_y(1))}
     down = {0: remote(page_ref, home, at_y(3))}
-    pl.when(k == 1)(swapped.start)
     shared = [remote(page_ref, home, other)]
     for d in (1, 3, 2):
         along[d].wait_recv()
@@ -77,13 +96,17 @@
         up[d] = remote(here, here, at_y(1))
         down[d] = remote(here, here, at_y(3))
         shared.append(remote(here, here, other))
-    pl.when(k == 0)(kept.wait)
-    pl.when(k == 1)(swapped.wait_recv)
-    right = remote(wall_ref.at[x], wall_ref.at[x], at_x(1))
-    left = remote(wall_ref.at[x], wall_ref.at[x], at_x(3))
+    for copy in swapped:
+        pl.when(k == 1)(copy.wait_recv)
+    right = {}
+    left = {}
+    for n in (0, 1):
+        here = wall_ref.at[x, halves[n]]
+        right[n] = remote(w_ref.at[halves[n]], here, at_x(1), here)
+        here = wall_ref.at[x, halves[1 - n]]
+        left[1 - n] = remote(w_ref.at[halves[1 - n]], here, at_x(3), here)
     far = {}
     far_w = []
-    middle = w_ref.shape[0] // 2
     for d in (0, 1, 3, 2):
         dx = (4 - d) % 4
         up[d].wait_recv()
@@ -95,12 +118,13 @@
         far[1, d] = remote(here, here, at_y(3))
         shared.append(remote(piece(dx, 1), piece(dx, 1), other))
         if d == 3:
-            right.wait_recv()
-            here = wall_ref.at[lax.rem(x + 3, 4), pl.ds(0, middle)]
+            right[0].wait_recv()
+            here = wall_ref.at[lax.rem(x + 3, 4), halves[0]]
             far_w.append(remote(here, here, at_x(1)))
-            left.wait_recv()
-            here = wall_ref.at[lax.rem(x + 1, 4), pl.ds(middle, middle)]
+            left[1].wait_recv()
+            here = wall_ref.at[lax.rem(x + 1, 4), halves[1]]
             far_w.append(remote(here, here, at_x(3)))
+            far_w += [right[1], left[0]]
     for d in (0, 1, 3, 2):
         far[0, d].wait_recv()
         far[1, d].wait_recv()
@@ -112,11 +136,13 @@
         copy.wait_recv()
     for copy in copies:
         copy.wait_send()
-    pl.when(k == 1)(swapped.wait_send)
+    for copy in swapped:
+        pl.when(k == 1)(copy.wait_send)
+    pl.when(k == 0)(kept.wait)
     own.wait()
 
 
-GATHER_COPIES = 6 + 9 + 2 + 16 + 2 + 4
+GATHER_COPIES = 6 + 9 + 4 + 16 + 2 + 4
 
 
 def gather_pages(page_cache, weights):
@@ -131,7 +157,7 @@
         in_specs=[anywhere, anywhere],
         out_specs=(anywhere, anywhere),
         scratch_shapes=[
-            pltpu.SemaphoreType.DMA((4,)),
+            pltpu.SemaphoreType.DMA((6,)),
             pltpu.SemaphoreType.DMA((GATHER_COPIES,)),
             pltpu.SemaphoreType.DMA((GATHER_COPIES,)),
         ],
@@ -145,7 +171,8 @@
 
 
 def attention_kernel(
-    slot_ref, parent_ref, count_ref, lost_ref, q_ref, new_ref, kv_ref, out_ref, keys, values, query, top, total
+    slot_ref, parent_ref, count_ref, lost_ref, q_ref, new_ref, kv_ref, out_ref, keys, values, query, top, total,
+    score_a, score_b, peak_a, peak_b
 ):
     pages_here = q_ref.shape[0] // PAGE
     scale = math.log2(math.e) / math.sqrt(HD)
@@ -205,24 +232,34 @@
             top[:, lanes] = jnp.broadcast_to(highest, (8, width))
             total[:, lanes] = jnp.dot(with_ones, weight, preferred_element_type=jnp.float32)
 
-        def one_chunk(n, unused):
+        def look(n, score_ref, peak_ref):
             at = pl.ds(pl.multiple_of(n * CHUNK, CHUNK), CHUNK)
-            key = keys[at, :]
-            value = transposed(values[at, :])
-            for start, width in LANES:
-                lanes = pl.ds(start, width)
-                score = lax.dot_general(key, query[lanes, :], nt, preferred_element_type=jnp.float32)
-                before = top[:1, lanes]
-                highest = jnp.maximum(before, jnp.max(score, axis=0, keepdims=True))
-                weight = jnp.exp2(score * scale - highest * scale).astype(jnp.bfloat16)
-                factor = jnp.exp2((before - highest) * scale)
-                top[:, lanes] = jnp.broadcast_to(highest, (8, width))
-                total[:, lanes] = total[:, lanes] * factor + jnp.dot(
-                    value, weight, preferred_element_type=jnp.float32
-                )
+            score = lax.dot_general(keys[at, :], query[...], nt, preferred_element_type=jnp.float32)
+            score_ref[...] = score
+            peak_ref[...] = jnp.broadcast_to(jnp.max(score, axis=0, keepdims=True), peak_ref.shape)
+
+        def take(n, score_ref, peak_ref):
+            at = pl.ds(pl.multiple_of(n * CHUNK, CHUNK), CHUNK)
+            before = top[:1, :]
+            highest = jnp.maximum(before, peak_ref[:1, :])
+            weight = jnp.exp2(score_ref[...] * scale - highest * scale).astype(jnp.bfloat16)
+            factor = jnp.exp2((before - highest) * scale)
+            top[...] = jnp.broadcast_to(highest, top.shape)
+            total[...] = total[...] * factor + jnp.dot(
+                transposed(values[at, :]), weight, preferred_element_type=jnp.float32
+            )
+
+        def two_chunks(n, unused):
+            look(2 * n + 1, score_b, peak_b)
+            take(2 * n, score_a, peak_a)
+            look(2 * n + 2, score_a, peak_a)
+            take(2 * n + 1, score_b, peak_b)
             return unused
 
-        lax.fori_loop(0, (filled + CHUNK - 1) // CHUNK, one_chunk, 0)
+        chunks = (filled + CHUNK - 1) // CHUNK
+        look(0, score_a, peak_a)
+        lax.fori_loop(0, chunks // 2, two_chunks, 0)
+        pl.when(chunks % 2 == 1)(lambda: take(chunks - 1, score_a, peak_a))
         for h in range(GROUP):
             lanes = pl.ds(h * PAGE, PAGE)
             out_ref[h * HD : (h + 1) * HD, rows] = (total[:HD, lanes] / total[HD : HD + 1, lanes]).astype(
@@ -243,29 +280,35 @@
         in_specs=[smem] * 4 + [vmem] * 3,
         out_specs=vmem,
         scratch_shapes=[
-            pltpu.VMEM((rows + CHUNK, HD), jnp.bfloat16),
+            pltpu.VMEM((rows + 2 * CHUNK, HD), jnp.bfloat16),
             pltpu.VMEM((rows + CHUNK, 2 * HD), jnp.bfloat16),
             pltpu.VMEM((GROUP * PAGE, HD), jnp.bfloat16),
             pltpu.VMEM((8, GROUP * PAGE), jnp.float32),
             pltpu.VMEM((HD + EXTRA, GROUP * PAGE), jnp.float32),
+            pltpu.VMEM((CHUNK, GROUP * PAGE), jnp.float32),
+            pltpu.VMEM((CHUNK, GROUP * PAGE), jnp.float32),
+            pltpu.VMEM((8, GROUP * PAGE), jnp.float32),
+            pltpu.VMEM((8, GROUP * PAGE), jnp.float32),
         ],
         compiler_params=pltpu.CompilerParams(vmem_limit_bytes=VMEM_LIMIT),
         name="attend",
     )(page_slot, parent, valid_count, lost_parent, queries, new_kv, kv)
 
 
-PARTS = [((0, 0), (0, 1), 0), ((0, 1), (0, 1), 0)]
-PARTS += [((dy, dk), (0,), 2) for dy in (1, 3) for dk in (0, 1)]
-PARTS += [((dy, dk), (1,), 3) for dy in (1, 3) for dk in (0, 1)]
-PARTS += [((2, dk), (0,), 3) for dk in (0, 1)]
-PARTS += [((2, dk), (1,), 4) for dk in (0, 1)]
+GROUPS = [
+    (((0, 0, 0), (0, 0, 1)), 0.0),
+    (((0, 1, 0), (0, 1, 1)), 0.4),
+    (((1, 0, 0), (3, 0, 0)), 1.3),
+    (((1, 1, 0), (3, 1, 0)), 1.8),
+    (((1, 0, 1), (3, 0, 1)), 2.3),
+    (((1, 1, 1), (3, 1, 1)), 2.7),
+    (((2, 0, 0), (2, 1, 0)), 2.9),
+    (((2, 0, 1), (2, 1, 1)), 3.5),
+]
 STEPS = 5
-WAVES = [
-    (block, sides, wave - delay)
-    for wave in range(STEPS + 4)
-    for block, sides, delay in PARTS
-    if 0 <= wave - delay < STEPS
-]
+EVENTS = [(start - 0.05, parts, None) for parts, start in GROUPS]
+EVENTS += [(start + step, parts, step) for parts, start in GROUPS for step in range(STEPS)]
+EVENTS.sort(key=lambda event: event[0])
 EVEN = ((4, None, 0), (-2, 2, 2), (2, 0, 1))
 ODD = ((-3, None, 2), (3, 0, 0), (-1, 2, 3), (1, 1, 1))
 
@@ -282,7 +325,7 @@
     columns = w_ref.shape[0] // 4
     width = att_ref.shape[1] // 2
     lanes = (pl.ds(0, width), pl.ds(width, width))
-    mine = lax.rem(y, 2) * 2 + k
+    mine = lax.rem(y + k, 2) * 2 + k
     odd = lax.rem(t + lax.div(y, 2) + k, 2)
     barrier = pltpu.get_barrier_semaphore()
     others = [(dy, dk) for dy in range(4) for dk in range(2) if (dy, dk) != (0, 0)]
@@ -303,11 +346,15 @@
         return copy
 
     shared = {}
-    for side in (0, 1):
+
+    def share_near(side):
         mine_here = att_ref.at[:, lanes[side]]
         shared[3, 0, side] = share(mine_here, 3, 0, side, holder(1, 0))
         shared[1, 0, side] = share(mine_here, 1, 0, side, holder(3, 0))
-        shared[0, 1, side] = share(mine_here, 0, 1, side, holder(0, 1))
+
+    share_near(0)
+    for side in (0, 1):
+        shared[0, 1, side] = share(att_ref.at[:, lanes[side]], 0, 1, side, holder(0, 1))
 
     def need(dy, dk, side):
         if (dy, dk) == (0, 0):
@@ -321,8 +368,8 @@
     def long_way(dk):
         return (1 - 2 * k) * (1 - 2 * dk)
 
-    def hop(block, i, side, arm, slot):
-        dy, dk = block
+    def hop(part, i, arm, slot):
+        dy, dk, side = part
         step = long_way(dk) if arm > 0 else -long_way(dk)
         return pltpu.make_async_remote_copy(
             outgoing.at[dy, dk, i, side],
@@ -333,16 +380,16 @@
             device_id_type=MESH,
         )
 
-    def arrived(block, slot, side):
-        dy, dk = block
+    def arrived(part, slot):
+        dy, dk, side = part
         spot = incoming.at[dy, dk, slot, side]
         pltpu.make_async_copy(spot, spot, z_recv.at[dy, dk, slot, side]).wait()
         return incoming[dy, dk, slot, side].astype(jnp.float32)
 
     spot = pl.ds(pl.multiple_of(mine * columns, 16), columns)
 
-    def result(block, side):
-        dy, dk = block
+    def result(part):
+        dy, dk, side = part
         return pltpu.make_async_remote_copy(
             outgoing.at[dy, dk, 3, side],
             out_ref.at[spot, lanes[side]],
@@ -352,53 +399,55 @@
             device_id_type=MESH,
         )
 
-    def term(block, distance, side):
-        dy, dk = block
+    def term(part, distance):
+        dy, dk, side = part
         target = lax.rem(t + long_way(dk) * distance + 8, 8)
         at = pl.ds(pl.multiple_of(lax.div(target, 2) * columns, 32), columns)
-        return terms[dy, dk, at, side * width : (side + 1) * width]
-
-    def pass_on(block, sides, i, table):
-        dy, dk = block
+        return terms[dy, dk, side, at, :]
+
+    def pass_on(parts, i, table):
         distance, source, slot = table[i]
-        for side in sides:
-            total = term(block, distance, side)
+        for part in parts:
+            dy, dk, side = part
+            total = term(part, distance)
             if source is not None:
-                total = total + arrived(block, source, side)
+                total = total + arrived(part, source)
             outgoing[dy, dk, i, side] = total.astype(jnp.bfloat16)
-            hop(block, i, side, distance, slot).start()
-
-    def finish(block, sides):
-        dy, dk = block
-        for side in sides:
-            total = term(block, 0, side) + arrived(block, 3, side) + arrived(block, 1, side)
-            if block == (0, 0):
+            hop(part, i, distance, slot).start()
+
+    def finish(parts):
+        for part in parts:
+            dy, dk, side = part
+            total = term(part, 0) + arrived(part, 3) + arrived(part, 1)
+            if (dy, dk) == (0, 0):
                 out_ref[spot, lanes[side]] = total.astype(jnp.bfloat16)
             else:
                 outgoing[dy, dk, 3, side] = total.astype(jnp.bfloat16)
-                result(block, side).start()
-
-    for block, sides, i in WAVES:
-        dy, dk = block
-        if i == 0:
-            for side in sides:
-                need(dy, dk, side)
-            if block == (0, 0):
-                rows = att_ref[...]
-            elif len(sides) == 2:
-                rows = jnp.concatenate([peers[dy, dk, 0], peers[dy, dk, 1]], axis=1)
-            else:
-                rows = peers[dy, dk, sides[0]]
-            start = sides[0] * width
-            terms[dy, dk, :, start : start + len(sides) * width] = jnp.dot(
-                w_ref[...], rows, preferred_element_type=jnp.float32
-            )
+                result(part).start()
+
+    def multiply(parts):
+        for part in parts:
+            need(*part)
+        if parts[0][:2] == (0, 0):
+            rows = att_ref[...]
+        else:
+            rows = jnp.concatenate([peers[part] for part in parts], axis=1)
+        products = jnp.dot(w_ref[...], rows, preferred_element_type=jnp.float32)
+        for n, (dy, dk, side) in enumerate(parts):
+            terms[dy, dk, side] = products[:, n * width : (n + 1) * width]
+
+    for unused_time, parts, i in EVENTS:
+        if i is None:
+            if parts[0][0] == 1 and (1, 0, 1) not in shared:
+                share_near(1)
+            multiply(parts)
+            continue
         if i < 4:
-            pl.when(odd == 1)(lambda block=block, sides=sides, i=i: pass_on(block, sides, i, ODD))
+            pl.when(odd == 1)(lambda parts=parts, i=i: pass_on(parts, i, ODD))
         if i < 3:
-            pl.when(odd == 0)(lambda block=block, sides=sides, i=i: pass_on(block, sides, i, EVEN))
+            pl.when(odd == 0)(lambda parts=parts, i=i: pass_on(parts, i, EVEN))
         if i == 4:
-            pl.when(odd == 0)(lambda block=block, sides=sides: finish(block, sides))
+            pl.when(odd == 0)(lambda parts=parts: finish(parts))
 
     for n in range(4):
 
@@ -411,20 +460,19 @@
     for copy in shared.values():
         copy.wait_send()
 
-    def drain(block, table):
+    def drain(part, table):
         for i, (distance, source, slot) in enumerate(table):
-            for side in (0, 1):
-                hop(block, i, side, distance, slot).wait_send()
-
-    for block in [(0, 0)] + others:
-        pl.when(odd == 1)(lambda block=block: drain(block, ODD))
-
-        @pl.when(odd == 0)
-        def _(block=block):
-            drain(block, EVEN)
-            if block != (0, 0):
-                result(block, 0).wait_send()
-                result(block, 1).wait_send()
+            hop(part, i, distance, slot).wait_send()
+
+    for parts, unused_start in GROUPS:
+        for part in parts:
+            pl.when(odd == 1)(lambda part=part: drain(part, ODD))
+
+            @pl.when(odd == 0)
+            def _(part=part):
+                drain(part, EVEN)
+                if part[:2] != (0, 0):
+                    result(part).wait_send()
 
 
 def project(attended, weights):
@@ -438,7 +486,7 @@
         out_specs=vmem,
         scratch_shapes=[
             pltpu.VMEM((4, 2, 2, depth, rows // 2), jnp.bfloat16),
-            pltpu.VMEM((4, 2, 4 * columns, rows), jnp.float32),
+            pltpu.VMEM((4, 2, 2, 4 * columns, rows // 2), jnp.float32),
             pltpu.VMEM((4, 2, 4, 2, columns, rows // 2), jnp.bfloat16),
             pltpu.VMEM((4, 2, 4, 2, columns, rows // 2), jnp.bfloat16),
             pltpu.SemaphoreType.DMA((4, 2, 2)),

time: 116 us -> 99.2 us (0.86)
  Pallas kernels: 114 us -> 96.9 us
    pallas_call x1, Pallas kernels: 36.5 us -> 30.4 us  [gather_pages(): pl.pallas_call(gather_kernel, out_shape=(jax.ShapeDtypeStruct((2, 4, 4, 2...]
    pallas_call x1, Pallas kernels: 14.2 us -> 8.53 us  [attend(): pl.pallas_call(attention_kernel, out_shape=jax.ShapeDtypeStruct(queries.s...]
    pallas_call x1, Pallas kernels: 63.2 us -> 57.9 us  [project(): pl.pallas_call(project_kernel, out_shape=jax.ShapeDtypeStruct((4 * column...]
where the time goes in v5:
time: 99.2 us; the launch traced here: 98.9 us
  Pallas kernels  96.9 us (98%)
  local copies, waits for them, and re-layouts  1.99 us (2%)
    pallas_call x1, Pallas kernels, project(): pl.pallas_call(project_kernel, out_shape=jax.ShapeDtypeStruct((4 * column...  57.9 us
    pallas_call x1, Pallas kernels, gather_pages(): pl.pallas_call(gather_kernel, out_shape=(jax.ShapeDtypeStruct((2, 4, 4, 2...  30.4 us
    pallas_call x1, Pallas kernels, attend(): pl.pallas_call(attention_kernel, out_shape=jax.ShapeDtypeStruct(queries.s...  8.53 us
    transpose x1, local copies, waits for them, and re-layouts, per_device(): return project(attended, weights.reshape(-1, weights.shape[2])).T  1.99 us

profile of v5, /device:TPU:33, one launch (start us, length us, event | category | flops | bytes accessed | tf_op | source)
XLA Modules:
  0.0 98.9 jit_solution(3545096731254998678)
XLA Ops:
  0.0 30.4 %gather_pages.1 = (bf16[2,4,4,2,256,128]{5,4,3,2,1,0:T(8,128)(2,1)}, bf16[4,224,896]{2,1,0:T(8,128)(2,1)}) custom-call(bf16[2,256,128]{2,1,0:T(8,128)(2,1)} %page_ref.1, bf16[224,896]{1,0:T(8,128)(2,1)} %bitcast.7), custom_call_target="tpu_custom_call" | custom-call | tf_op jit(solution)/shard_map/gather_pages/pallas_call | solution.py:151
  30.4 8.5 %attend.1.att_ref = bf16[896,256]{1,0:T(8,128)(2,1)} custom-call(s32[64]{0:T(128)} %slot_ref.1, s32[64]{0:T(128)} %parent_ref.1, s32[64]{0:T(128)} %count_ref.1, s32[64]{0:T(128)} %lost_ref.1, bf16[256,896]{1,0:T(8,128)(2,1)} %q_ref.1, bf16[2,256,128]{2,1,0:T(8,128)(2,1)} %new_ref.1, bf16[2,8192,128]{2,1,0:T(8,128)(2,1)} %bitcast.4), custom_call_target="tpu_custom_call" | custom-call | tf_op jit(solution)/shard_map/attend/pallas_call | solution.py:277
  39.0 57.9 %project.1 = bf16[896,256]{1,0:T(8,128)(2,1)} custom-call(bf16[896,256]{1,0:T(8,128)(2,1)} %attend.1.att_ref, bf16[896,896]{1,0:T(8,128)(2,1)} %bitcast.6), custom_call_target="tpu_custom_call" | custom-call | tf_op jit(solution)/shard_map/project/pallas_call | solution.py:482
  96.9 2.0 %copy.9 = bf16[256,896]{1,0:T(8,128)(2,1)} copy(bf16[256,896]{0,1:T(8,128)(2,1)} %bitcast.5) | data formatting | bytes 917504 | tf_op jit(solution)/shard_map/transpose | solution.py:512

commit v6 on v5

--- a/solution.py
+++ b/solution.py
@@ -174,100 +174,94 @@
     slot_ref, parent_ref, count_ref, lost_ref, q_ref, new_ref, kv_ref, out_ref, keys, values, query, top, total,
     score_a, score_b, peak_a, peak_b
 ):
-    pages_here = q_ref.shape[0] // PAGE
     scale = math.log2(math.e) / math.sqrt(HD)
-    base = lax.axis_index("ctx") * pages_here
+    j = pl.program_id(0)
+    base = lax.axis_index("ctx") * pl.num_programs(0)
     token = lax.broadcasted_iota(jnp.int32, (16, HD), 0)
     nt = (((1,), (1,)), ((), ()))
 
     def transposed(block):
         return block.T[: HD + EXTRA]
 
-    def one_lost(j, unused):
-        rows = pl.ds(pl.multiple_of(j * PAGE, PAGE), PAGE)
-
-        def append(state):
-            page, filled = state
-            count = count_ref[page]
-            first = slot_ref[page] * PAGE
-            at = pl.ds(pl.multiple_of(first, PAGE), PAGE)
-            to = pl.ds(pl.multiple_of(filled, 16), PAGE)
-            keys[to, :] = kv_ref[0, at, :]
-            values[to, :HD] = kv_ref[1, at, :]
-            values[to, HD:] = jnp.ones((PAGE, HD), jnp.bfloat16)
-            last = ((count - 1) // 16) * 16
-            kept = token + last < count
-            at = pl.ds(pl.multiple_of(first + last, 16), 16)
-            to = pl.ds(pl.multiple_of(filled + last, 16), 16)
-            lead = kv_ref[0, pl.ds(pl.multiple_of(first, PAGE), 16), :].astype(jnp.float32)[:1, :]
-            keys[to, :] = jnp.where(kept, kv_ref[0, at, :].astype(jnp.float32), lead).astype(jnp.bfloat16)
-            values[to, :HD] = jnp.where(kept, kv_ref[1, at, :].astype(jnp.float32), 0.0).astype(jnp.bfloat16)
-            values[to, HD:] = kept.astype(jnp.float32).astype(jnp.bfloat16)
-            return parent_ref[page], filled + last + 16
-
-        unused_page, filled = lax.while_loop(
-            lambda state: state[0] >= 0, append, (lost_ref[base + j], jnp.int32(0))
-        )
-        tail = pl.ds(pl.multiple_of(filled, 16), CHUNK)
-        lead = keys[:16, :].astype(jnp.float32)[:1, :]
-        keys[tail, :] = jnp.broadcast_to(lead, (CHUNK, HD)).astype(jnp.bfloat16)
-        values[tail, :] = jnp.zeros((CHUNK, 2 * HD), jnp.bfloat16)
-        for h in range(GROUP):
-            query[h * PAGE : (h + 1) * PAGE, :] = q_ref[rows, h * HD : (h + 1) * HD]
-
-        with_ones = transposed(
-            jnp.concatenate([new_ref[1, rows, :], jnp.ones((PAGE, HD), jnp.bfloat16)], axis=1)
-        )
-        for start, width in LANES:
-            lanes = pl.ds(start, width)
-            score = lax.dot_general(
-                new_ref[0, rows, :], query[lanes, :], nt, preferred_element_type=jnp.float32
-            )
-            k_at = lax.broadcasted_iota(jnp.int32, (PAGE, width), 0)
-            q_at = lax.broadcasted_iota(jnp.int32, (PAGE, width), 1) % PAGE
-            seen = k_at <= q_at
-            score = jnp.where(seen, score, -1e30)
-            highest = jnp.max(score, axis=0, keepdims=True)
-            weight = jnp.where(seen, jnp.exp2(score * scale - highest * scale), 0.0).astype(jnp.bfloat16)
-            top[:, lanes] = jnp.broadcast_to(highest, (8, width))
-            total[:, lanes] = jnp.dot(with_ones, weight, preferred_element_type=jnp.float32)
-
-        def look(n, score_ref, peak_ref):
-            at = pl.ds(pl.multiple_of(n * CHUNK, CHUNK), CHUNK)
-            score = lax.dot_general(keys[at, :], query[...], nt, preferred_element_type=jnp.float32)
-            score_ref[...] = score
-            peak_ref[...] = jnp.broadcast_to(jnp.max(score, axis=0, keepdims=True), peak_ref.shape)
-
-        def take(n, score_ref, peak_ref):
-            at = pl.ds(pl.multiple_of(n * CHUNK, CHUNK), CHUNK)
-            before = top[:1, :]
-            highest = jnp.maximum(before, peak_ref[:1, :])
-            weight = jnp.exp2(score_ref[...] * scale - highest * scale).astype(jnp.bfloat16)
-            factor = jnp.exp2((before - highest) * scale)
-            top[...] = jnp.broadcast_to(highest, top.shape)
-            total[...] = total[...] * factor + jnp.dot(
-                transposed(values[at, :]), weight, preferred_element_type=jnp.float32
-            )
-
-        def two_chunks(n, unused):
-            look(2 * n + 1, score_b, peak_b)
-            take(2 * n, score_a, peak_a)
-            look(2 * n + 2, score_a, peak_a)
-            take(2 * n + 1, score_b, peak_b)
-            return unused
-
-        chunks = (filled + CHUNK - 1) // CHUNK
-        look(0, score_a, peak_a)
-        lax.fori_loop(0, chunks // 2, two_chunks, 0)
-        pl.when(chunks % 2 == 1)(lambda: take(chunks - 1, score_a, peak_a))
-        for h in range(GROUP):
-            lanes = pl.ds(h * PAGE, PAGE)
-            out_ref[h * HD : (h + 1) * HD, rows] = (total[:HD, lanes] / total[HD : HD + 1, lanes]).astype(
-                jnp.bfloat16
-            )
+    def append(state):
+        page, filled = state
+        count = count_ref[page]
+        first = slot_ref[page] * PAGE
+        at = pl.ds(pl.multiple_of(first, PAGE), PAGE)
+        to = pl.ds(pl.multiple_of(filled, 16), PAGE)
+        keys[to, :] = kv_ref[0, at, :]
+        values[to, :HD] = kv_ref[1, at, :]
+        values[to, HD:] = jnp.ones((PAGE, HD), jnp.bfloat16)
+        last = ((count - 1) // 16) * 16
+        kept = token + last < count
+        at = pl.ds(pl.multiple_of(first + last, 16), 16)
+        to = pl.ds(pl.multiple_of(filled + last, 16), 16)
+        lead = kv_ref[0, pl.ds(pl.multiple_of(first, PAGE), 16), :].astype(jnp.float32)[:1, :]
+        keys[to, :] = jnp.where(kept, kv_ref[0, at, :].astype(jnp.float32), lead).astype(jnp.bfloat16)
+        values[to, :HD] = jnp.where(kept, kv_ref[1, at, :].astype(jnp.float32), 0.0).astype(jnp.bfloat16)
+        values[to, HD:] = kept.astype(jnp.float32).astype(jnp.bfloat16)
+        return parent_ref[page], filled + last + 16
+
+    unused_page, filled = lax.while_loop(
+        lambda state: state[0] >= 0, append, (lost_ref[base + j], jnp.int32(0))
+    )
+    tail = pl.ds(pl.multiple_of(filled, 16), CHUNK)
+    lead = keys[:16, :].astype(jnp.float32)[:1, :]
+    keys[tail, :] = jnp.broadcast_to(lead, (CHUNK, HD)).astype(jnp.bfloat16)
+    values[tail, :] = jnp.zeros((CHUNK, 2 * HD), jnp.bfloat16)
+    for h in range(GROUP):
+        query[h * PAGE : (h + 1) * PAGE, :] = q_ref[:, h * HD : (h + 1) * HD]
+
+    with_ones = transposed(
+        jnp.concatenate([new_ref[1], jnp.ones((PAGE, HD), jnp.bfloat16)], axis=1)
+    )
+    for start, width in LANES:
+        lanes = pl.ds(start, width)
+        score = lax.dot_general(
+            new_ref[0], query[lanes, :], nt, preferred_element_type=jnp.float32
+        )
+        k_at = lax.broadcasted_iota(jnp.int32, (PAGE, width), 0)
+        q_at = lax.broadcasted_iota(jnp.int32, (PAGE, width), 1) % PAGE
+        seen = k_at <= q_at
+        score = jnp.where(seen, score, -1e30)
+        highest = jnp.max(score, axis=0, keepdims=True)
+        weight = jnp.where(seen, jnp.exp2(score * scale - highest * scale), 0.0).astype(jnp.bfloat16)
+        top[:, lanes] = jnp.broadcast_to(highest, (8, width))
+        total[:, lanes] = jnp.dot(with_ones, weight, preferred_element_type=jnp.float32)
+
+    def look(n, score_ref, peak_ref):
+        at = pl.ds(pl.multiple_of(n * CHUNK, CHUNK), CHUNK)
+        score = lax.dot_general(keys[at, :], query[...], nt, preferred_element_type=jnp.float32)
+        score_ref[...] = score
+        peak_ref[...] = jnp.broadcast_to(jnp.max(score, axis=0, keepdims=True), peak_ref.shape)
+
+    def take(n, score_ref, peak_ref):
+        at = pl.ds(pl.multiple_of(n * CHUNK, CHUNK), CHUNK)
+        before = top[:1, :]
+        highest = jnp.maximum(before, peak_ref[:1, :])
+        weight = jnp.exp2(score_ref[...] * scale - highest * scale).astype(jnp.bfloat16)
+        factor = jnp.exp2((before - highest) * scale)
+        top[...] = jnp.broadcast_to(highest, top.shape)
+        total[...] = total[...] * factor + jnp.dot(
+            transposed(values[at, :]), weight, preferred_element_type=jnp.float32
+        )
+
+    def two_chunks(n, unused):
+        look(2 * n + 1, score_b, peak_b)
+        take(2 * n, score_a, peak_a)
+        look(2 * n + 2, score_a, peak_a)
+        take(2 * n + 1, score_b, peak_b)
         return unused
 
-    lax.fori_loop(0, pages_here, one_lost, 0)
+    chunks = (filled + CHUNK - 1) // CHUNK
+    look(0, score_a, peak_a)
+    lax.fori_loop(0, chunks // 2, two_chunks, 0)
+    pl.when(chunks % 2 == 1)(lambda: take(chunks - 1, score_a, peak_a))
+    for h in range(GROUP):
+        lanes = pl.ds(h * PAGE, PAGE)
+        out_ref[h * HD : (h + 1) * HD, :] = (total[:HD, lanes] / total[HD : HD + 1, lanes]).astype(
+            jnp.bfloat16
+        )
 
 
 def attend(queries, new_kv, kv, page_slot, parent, valid_count, lost_parent):
@@ -277,8 +271,14 @@
     return pl.pallas_call(
         attention_kernel,
         out_shape=jax.ShapeDtypeStruct(queries.shape[::-1], jnp.bfloat16),
-        in_specs=[smem] * 4 + [vmem] * 3,
-        out_specs=vmem,
+        grid=(queries.shape[0] // PAGE,),
+        in_specs=[smem] * 4
+        + [
+            pl.BlockSpec((PAGE, queries.shape[1]), lambda j: (j, 0)),
+            pl.BlockSpec((2, PAGE, HD), lambda j: (0, j, 0)),
+            vmem,
+        ],
+        out_specs=pl.BlockSpec((queries.shape[1], PAGE), lambda j: (0, j)),
         scratch_shapes=[
             pltpu.VMEM((rows + 2 * CHUNK, HD), jnp.bfloat16),
             pltpu.VMEM((rows + CHUNK, 2 * HD), jnp.bfloat16),
@@ -314,7 +314,8 @@
 
 
 def project_kernel(
-    att_ref, w_ref, out_ref, peers, terms, outgoing, incoming, a_send, a_recv, z_send, z_recv, f_send, f_recv
+    own_ref, all_ref, out_ref, att_ref, w_ref, peers, terms, outgoing, incoming, load_sem,
+    a_send, a_recv, z_send, z_recv, f_send, f_recv
 ):
     x, y, k, t = place()
     here = ctx_of(x, y, k)
@@ -322,6 +323,12 @@
     def holder(dy, dk):
         return (ctx_of(x, lax.rem(y + dy, 4), k if dk == 0 else 1 - k), t)
 
+    loads = [
+        pltpu.make_async_copy(own_ref, att_ref, load_sem.at[0]),
+        pltpu.make_async_copy(all_ref, w_ref, load_sem.at[1]),
+    ]
+    for copy in loads:
+        copy.start()
     columns = w_ref.shape[0] // 4
     width = att_ref.shape[1] // 2
     lanes = (pl.ds(0, width), pl.ds(width, width))
@@ -348,13 +355,13 @@
     shared = {}
 
     def share_near(side):
-        mine_here = att_ref.at[:, lanes[side]]
+        mine_here = own_ref.at[:, lanes[side]]
         shared[3, 0, side] = share(mine_here, 3, 0, side, holder(1, 0))
         shared[1, 0, side] = share(mine_here, 1, 0, side, holder(3, 0))
 
     share_near(0)
     for side in (0, 1):
-        shared[0, 1, side] = share(att_ref.at[:, lanes[side]], 0, 1, side, holder(0, 1))
+        shared[0, 1, side] = share(own_ref.at[:, lanes[side]], 0, 1, side, holder(0, 1))
 
     def need(dy, dk, side):
         if (dy, dk) == (0, 0):
@@ -436,6 +443,8 @@
         for n, (dy, dk, side) in enumerate(parts):
             terms[dy, dk, side] = products[:, n * width : (n + 1) * width]
 
+    for copy in loads:
+        copy.wait()
     for unused_time, parts, i in EVENTS:
         if i is None:
             if parts[0][0] == 1 and (1, 0, 1) not in shared:
@@ -482,13 +491,16 @@
     return pl.pallas_call(
         project_kernel,
         out_shape=jax.ShapeDtypeStruct((4 * columns, rows), jnp.bfloat16),
-        in_specs=[vmem, vmem],
+        in_specs=[pl.BlockSpec(memory_space=pl.ANY)] * 2,
         out_specs=vmem,
         scratch_shapes=[
+            pltpu.VMEM((depth, rows), jnp.bfloat16),
+            pltpu.VMEM(weights.shape, jnp.bfloat16),
             pltpu.VMEM((4, 2, 2, depth, rows // 2), jnp.bfloat16),
             pltpu.VMEM((4, 2, 2, 4 * columns, rows // 2), jnp.float32),
             pltpu.VMEM((4, 2, 4, 2, columns, rows // 2), jnp.bfloat16),
             pltpu.VMEM((4, 2, 4, 2, columns, rows // 2), jnp.bfloat16),
+            pltpu.SemaphoreType.DMA((2,)),
             pltpu.SemaphoreType.DMA((4, 2, 2)),
             pltpu.SemaphoreType.DMA((4, 2, 2)),
             pltpu.SemaphoreType.DMA((4, 2, 4, 2)),

time: 99.2 us -> 98.9 us (level)
    pallas_call x1, Pallas kernels: 57.9 us -> 56.6 us  [project(): pl.pallas_call(project_kernel, out_shape=jax.ShapeDtypeStruct((4 * column...]
    pallas_call x1, Pallas kernels: 8.53 us -> 9.79 us  [attend(): pl.pallas_call(attention_kernel, out_shape=jax.ShapeDtypeStruct(queries.s...]
where the time goes in v6:
time: 98.9 us; the launch traced here: 98.8 us
  Pallas kernels  96.8 us (98%)
  local copies, waits for them, and re-layouts  1.99 us (2%)
    pallas_call x1, Pallas kernels, project(): pl.pallas_call(project_kernel, out_shape=jax.ShapeDtypeStruct((4 * column...  56.6 us
    pallas_call x1, Pallas kernels, gather_pages(): pl.pallas_call(gather_kernel, out_shape=(jax.ShapeDtypeStruct((2, 4, 4, 2...  30.4 us
    pallas_call x1, Pallas kernels, attend(): pl.pallas_call(attention_kernel, out_shape=jax.ShapeDtypeStruct(queries.s...  9.79 us
    transpose x1, local copies, waits for them, and re-layouts, per_device(): return project(attended, weights.reshape(-1, weights.shape[2])).T  1.99 us

profile of v6, /device:TPU:33, one launch (start us, length us, event | category | flops | bytes accessed | tf_op | source)
XLA Modules:
  0.0 98.8 jit_solution(7038674731310540690)
XLA Ops:
  0.0 30.4 %gather_pages.1 = (bf16[2,4,4,2,256,128]{5,4,3,2,1,0:T(8,128)(2,1)}, bf16[4,224,896]{2,1,0:T(8,128)(2,1)}) custom-call(bf16[2,256,128]{2,1,0:T(8,128)(2,1)} %page_ref.1, bf16[224,896]{1,0:T(8,128)(2,1)} %bitcast.7), custom_call_target="tpu_custom_call" | custom-call | tf_op jit(solution)/shard_map/gather_pages/pallas_call | solution.py:151
  30.4 9.8 %attend.1.own_ref = bf16[896,256]{1,0:T(8,128)(2,1)} custom-call(s32[64]{0:T(128)} %slot_ref.1, s32[64]{0:T(128)} %parent_ref.1, s32[64]{0:T(128)} %count_ref.1, s32[64]{0:T(128)} %lost_ref.1, bf16[256,896]{1,0:T(8,128)(2,1)} %q_ref.1, bf16[2,256,128]{2,1,0:T(8,128)(2,1)} %new_ref.1, bf16[2,8192,128]{2,1,0:T(8,128)(2,1)} %bitcast.4), custom_call_target="tpu_custom_call" | custom-call | tf_op jit(solution)/shard_map/attend/pallas_call | solution.py:271
  40.2 56.6 %project.1 = bf16[896,256]{1,0:T(8,128)(2,1)} custom-call(bf16[896,256]{1,0:T(8,128)(2,1)} %attend.1.own_ref, bf16[896,896]{1,0:T(8,128)(2,1)} %bitcast.6), custom_call_target="tpu_custom_call" | custom-call | tf_op jit(solution)/shard_map/project/pallas_call | solution.py:491
  96.8 2.0 %copy.9 = bf16[256,896]{1,0:T(8,128)(2,1)} copy(bf16[256,896]{0,1:T(8,128)(2,1)} %bitcast.5) | data formatting | bytes 917504 | tf_op jit(solution)/shard_map/transpose | solution.py:524

commit v7 on v6

--- a/solution.py
+++ b/solution.py
@@ -372,12 +372,13 @@
                 shared[2, 0, side] = share(peers.at[dy, 0, side], 2, 0, side, holder(4 - dy, 0))
             shared[dy, 1, side] = share(peers.at[dy, 0, side], dy, 1, side, holder(0, 1))
 
-    def long_way(dk):
-        return (1 - 2 * k) * (1 - 2 * dk)
+    def long_way(part):
+        dy, dk, side = part
+        return (1 - 2 * k) * (-1 if (dk + side + (dy == 3)) % 2 else 1)
 
     def hop(part, i, arm, slot):
         dy, dk, side = part
-        step = long_way(dk) if arm > 0 else -long_way(dk)
+        step = long_way(part) if arm > 0 else -long_way(part)
         return pltpu.make_async_remote_copy(
             outgoing.at[dy, dk, i, side],
             incoming.at[dy, dk, slot, side],
@@ -408,7 +409,7 @@
 
     def term(part, distance):
         dy, dk, side = part
-        target = lax.rem(t + long_way(dk) * distance + 8, 8)
+        target = lax.rem(t + long_way(part) * distance + 8, 8)
         at = pl.ds(pl.multiple_of(lax.div(target, 2) * columns, 32), columns)
         return terms[dy, dk, side, at, :]
 

time: 98.9 us -> 97.6 us (0.987); the launches traced: 98.8 us -> 96.1 us
  Pallas kernels: 96.8 us -> 94.1 us
    pallas_call x1, Pallas kernels: 9.79 us -> 7.4 us  [attend(): pl.pallas_call(attention_kernel, out_shape=jax.ShapeDtypeStruct(queries.s...]
where the time goes in v7:
time: 97.6 us; the launch traced here: 96.1 us
  Pallas kernels  94.1 us (96%)
  local copies, waits for them, and re-layouts  1.99 us (2%)
    pallas_call x1, Pallas kernels, project(): pl.pallas_call(project_kernel, out_shape=jax.ShapeDtypeStruct((4 * column...  56.3 us
    pallas_call x1, Pallas kernels, gather_pages(): pl.pallas_call(gather_kernel, out_shape=(jax.ShapeDtypeStruct((2, 4, 4, 2...  30.4 us
    pallas_call x1, Pallas kernels, attend(): pl.pallas_call(attention_kernel, out_shape=jax.ShapeDtypeStruct(queries.s...  7.4 us
    transpose x1, local copies, waits for them, and re-layouts, per_device(): return project(attended, weights.reshape(-1, weights.shape[2])).T  1.99 us

profile of v7, /device:TPU:33, one launch (start us, length us, event | category | flops | bytes accessed | tf_op | source)
XLA Modules:
  0.0 96.1 jit_solution(15024574135235562388)
XLA Ops:
  0.0 30.4 %gather_pages.1 = (bf16[2,4,4,2,256,128]{5,4,3,2,1,0:T(8,128)(2,1)}, bf16[4,224,896]{2,1,0:T(8,128)(2,1)}) custom-call(bf16[2,256,128]{2,1,0:T(8,128)(2,1)} %page_ref.1, bf16[224,896]{1,0:T(8,128)(2,1)} %bitcast.7), custom_call_target="tpu_custom_call" | custom-call | tf_op jit(solution)/shard_map/gather_pages/pallas_call | solution.py:151
  30.4 7.4 %attend.1.own_ref = bf16[896,256]{1,0:T(8,128)(2,1)} custom-call(s32[64]{0:T(128)} %slot_ref.1, s32[64]{0:T(128)} %parent_ref.1, s32[64]{0:T(128)} %count_ref.1, s32[64]{0:T(128)} %lost_ref.1, bf16[256,896]{1,0:T(8,128)(2,1)} %q_ref.1, bf16[2,256,128]{2,1,0:T(8,128)(2,1)} %new_ref.1, bf16[2,8192,128]{2,1,0:T(8,128)(2,1)} %bitcast.4), custom_call_target="tpu_custom_call" | custom-call | tf_op jit(solution)/shard_map/attend/pallas_call | solution.py:271
  37.8 56.3 %project.1 = bf16[896,256]{1,0:T(8,128)(2,1)} custom-call(bf16[896,256]{1,0:T(8,128)(2,1)} %attend.1.own_ref, bf16[896,896]{1,0:T(8,128)(2,1)} %bitcast.6), custom_call_target="tpu_custom_call" | custom-call | tf_op jit(solution)/shard_map/project/pallas_call | solution.py:492
  94.1 2.0 %copy.9 = bf16[256,896]{1,0:T(8,128)(2,1)} copy(bf16[256,896]{0,1:T(8,128)(2,1)} %bitcast.5) | data formatting | bytes 917504 | tf_op jit(solution)/shard_map/transpose | solution.py:525

commit v8 on v7

--- a/solution.py
+++ b/solution.py
@@ -296,14 +296,14 @@
 
 
 GROUPS = [
-    (((0, 0, 0), (0, 0, 1)), 0.0),
+    (((0, 0, 0), (0, 0, 1)), 0),
     (((0, 1, 0), (0, 1, 1)), 0.4),
     (((1, 0, 0), (3, 0, 0)), 1.3),
     (((1, 1, 0), (3, 1, 0)), 1.8),
     (((1, 0, 1), (3, 0, 1)), 2.3),
     (((1, 1, 1), (3, 1, 1)), 2.7),
     (((2, 0, 0), (2, 1, 0)), 2.9),
-    (((2, 0, 1), (2, 1, 1)), 3.5),
+    (((2, 0, 1), (2, 1, 1)), 3.2),
 ]
 STEPS = 5
 EVENTS = [(start - 0.05, parts, None) for parts, start in GROUPS]

time: 97.6 us -> 97.4 us (level)
    pallas_call x1, Pallas kernels: 56.3 us -> 53.7 us  [project(): pl.pallas_call(project_kernel, out_shape=jax.ShapeDtypeStruct((4 * column...]
    pallas_call x1, Pallas kernels: 7.4 us -> 9.37 us  [attend(): pl.pallas_call(attention_kernel, out_shape=jax.ShapeDtypeStruct(queries.s...]
where the time goes in v8:
time: 97.4 us; the launch traced here: 95.5 us
  Pallas kernels  93.5 us (96%)
  local copies, waits for them, and re-layouts  1.99 us (2%)
    pallas_call x1, Pallas kernels, project(): pl.pallas_call(project_kernel, out_shape=jax.ShapeDtypeStruct((4 * column...  53.7 us
    pallas_call x1, Pallas kernels, gather_pages(): pl.pallas_call(gather_kernel, out_shape=(jax.ShapeDtypeStruct((2, 4, 4, 2...  30.4 us
    pallas_call x1, Pallas kernels, attend(): pl.pallas_call(attention_kernel, out_shape=jax.ShapeDtypeStruct(queries.s...  9.37 us
    transpose x1, local copies, waits for them, and re-layouts, per_device(): return project(attended, weights.reshape(-1, weights.shape[2])).T  1.99 us

profile of v8, /device:TPU:33, one launch (start us, length us, event | category | flops | bytes accessed | tf_op | source)
XLA Modules:
  0.0 95.5 jit_solution(12227102985759126768)
XLA Ops:
  0.0 30.4 %gather_pages.1 = (bf16[2,4,4,2,256,128]{5,4,3,2,1,0:T(8,128)(2,1)}, bf16[4,224,896]{2,1,0:T(8,128)(2,1)}) custom-call(bf16[2,256,128]{2,1,0:T(8,128)(2,1)} %page_ref.1, bf16[224,896]{1,0:T(8,128)(2,1)} %bitcast.7), custom_call_target="tpu_custom_call" | custom-call | tf_op jit(solution)/shard_map/gather_pages/pallas_call | solution.py:151
  30.4 9.4 %attend.1.own_ref = bf16[896,256]{1,0:T(8,128)(2,1)} custom-call(s32[64]{0:T(128)} %slot_ref.1, s32[64]{0:T(128)} %parent_ref.1, s32[64]{0:T(128)} %count_ref.1, s32[64]{0:T(128)} %lost_ref.1, bf16[256,896]{1,0:T(8,128)(2,1)} %q_ref.1, bf16[2,256,128]{2,1,0:T(8,128)(2,1)} %new_ref.1, bf16[2,8192,128]{2,1,0:T(8,128)(2,1)} %bitcast.4), custom_call_target="tpu_custom_call" | custom-call | tf_op jit(solution)/shard_map/attend/pallas_call | solution.py:271
  39.8 53.7 %project.1 = bf16[896,256]{1,0:T(8,128)(2,1)} custom-call(bf16[896,256]{1,0:T(8,128)(2,1)} %attend.1.own_ref, bf16[896,896]{1,0:T(8,128)(2,1)} %bitcast.6), custom_call_target="tpu_custom_call" | custom-call | tf_op jit(solution)/shard_map/project/pallas_call | solution.py:492
  93.5 2.0 %copy.9 = bf16[256,896]{1,0:T(8,128)(2,1)} copy(bf16[256,896]{0,1:T(8,128)(2,1)} %bitcast.5) | data formatting | bytes 917504 | tf_op jit(solution)/shard_map/transpose | solution.py:525
